TPU v7x, 32 devices: a whole 2x2x4 slice. The times are simulated.
32 devices in a mesh: dp: 2 (over x), expert: 16 (over z, y, core).
Axes of the slice: x: 2, y: 2, z: 4, core: 2. Of those that a mesh axis runs over, the one named last changes fastest.
Arguments:
- tokens: bfloat16 [4096, 3584], P(('dp', 'expert')), may hold values from -6 to 6
- cotangent: bfloat16 [4096, 3584], P(('dp', 'expert')), may hold values from -0.09375 to 0.09375
- expert_ids: int32 [4096, 8], P(('dp', 'expert')), may hold values from 0 to 255, all different within a row; in each aligned block of 128 rows (0 to 127, 128 to 255, ...) at most 6 rows name the same one
- gates: bfloat16 [4096, 8], P(('dp', 'expert')), may hold values from 0.049804688 to 1
- swap_flags: int32 [8], replicated, may hold values 0 or 1
- gate_w: bfloat16 [16, 3584, 1024], P('expert', None, 'dp'), may hold values from -0.09375 to 0.09375
- up_w: bfloat16 [16, 3584, 1024], P('expert', None, 'dp'), may hold values from -0.09375 to 0.09375
- down_w: bfloat16 [16, 1024, 3584], P('expert', 'dp'), may hold values from -0.1875 to 0.1875
Outputs:
- grad_gate_w: bfloat16 [16, 3584, 1024], P('expert', None, 'dp')
- grad_up_w: bfloat16 [16, 3584, 1024], P('expert', None, 'dp')
- grad_down_w: bfloat16 [16, 1024, 3584], P('expert', 'dp')
- score_grad: float32 [4096, 8], P(('dp', 'expert'))
Inputs may be any that keep to these rules, and one draw needn't show every extreme that they name: `expert_ids`: among the 128 rows of one device no expert is named more than 6 times, a bound that some block reaches; the numbers of one row differ. `swap_flags`: 1 means that slots s and s + 8 trade their experts.
All inputs are finite; a program needn't handle non-finite values.
Results may differ from a plain program's by a relative error of at most 0.011.
Values may be sent and summed in bfloat16 or wider, within the bound.
No kernel may reach another device: no remote copies, remote signals or barrier semaphores. Data moves between devices by JAX's collectives and lax.ppermute only.
A program may use at most 128 MiB of HBM per device.

v0:
```python
import jax
import jax.numpy as jnp
from jax import lax
from jax.sharding import PartitionSpec as P

CAP = 6


def partner(block, axis, stride):
    count = lax.axis_size(axis)
    route = []
    for low in range(count):
        high = low | 1 << stride
        if high != low and high < count:
            route += [(low, high), (high, low)]
    return lax.ppermute(block, axis, route)


def body(tokens, cotangent, expert_ids, gates, swap_flags, gate_w, up_w, down_w):
    axis_len = lax.axis_size("expert")
    half_axis = axis_len // 2
    pair_bit = axis_len.bit_length() - 2
    own_slot = lax.axis_index("expert")
    tok_count = tokens.shape[0]
    top_count = expert_ids.shape[1]
    width = tokens.shape[1]
    flat_ids = expert_ids.reshape(-1)
    choice_count = flat_ids.shape[0]
    valid = flat_ids < axis_len
    pair_index = jnp.arange(half_axis, dtype=jnp.int32)
    flag_of = jnp.sum(
        jnp.where((flat_ids % half_axis)[:, None] == pair_index[None, :], swap_flags[None, :], 0),
        axis=1,
    )
    own_flag = jnp.sum(jnp.where(pair_index == own_slot % half_axis, swap_flags, 0))
    target = jnp.where(flag_of == 1, jnp.bitwise_xor(flat_ids, half_axis), flat_ids)
    target = jnp.where(valid, target, 0)
    onehot = jnp.where(
        (target[:, None] == jnp.arange(axis_len, dtype=jnp.int32)[None, :]) & valid[:, None], 1, 0
    ).astype(jnp.int32)
    ranks = jnp.sum(jnp.cumsum(onehot, axis=0) * onehot, axis=1) - 1
    slot_count = axis_len * CAP
    slots = jnp.where(valid, target * CAP + ranks, slot_count)
    source = (
        jnp.full((slot_count,), choice_count, jnp.int32)
        .at[slots]
        .set(jnp.arange(choice_count, dtype=jnp.int32), mode="drop")
    )
    token_index = source // top_count
    padded_x = jnp.concatenate([tokens, jnp.zeros((1, width), tokens.dtype)], axis=0)
    padded_dy = jnp.concatenate([cotangent, jnp.zeros((1, width), cotangent.dtype)], axis=0)
    padded_g = jnp.concatenate([gates.reshape(-1), jnp.zeros((1,), gates.dtype)], axis=0)
    send_x = padded_x[token_index].reshape(axis_len, CAP, width)
    send_dy = padded_dy[token_index].reshape(axis_len, CAP, width)
    send_g = padded_g[source].reshape(axis_len, CAP)
    recv_x, recv_dy, recv_g = (
        lax.all_to_all(send_x, "expert", split_axis=0, concat_axis=0, tiled=True),
        lax.all_to_all(send_dy, "expert", split_axis=0, concat_axis=0, tiled=True),
        lax.all_to_all(send_g, "expert", split_axis=0, concat_axis=0, tiled=True),
    )
    w_gate = gate_w[0]
    w_up = up_w[0]
    w_down = down_w[0]
    other_gate, other_up, other_down = partner((gate_w, up_w, down_w), "expert", pair_bit)
    taken = own_flag == 1
    w_gate = jnp.where(taken, other_gate[0], w_gate)
    w_up = jnp.where(taken, other_up[0], w_up)
    w_down = jnp.where(taken, other_down[0], w_down)
    contract = (((0,), (0,)), ((), ()))
    part_x = lax.all_gather(recv_x, "dp", axis=0, tiled=True)
    part_dy = lax.all_gather(recv_dy, "dp", axis=0, tiled=True)
    part_g = lax.all_gather(recv_g, "dp", axis=0, tiled=True)
    block_count = part_x.shape[0]
    row_x = part_x.reshape(-1, width)
    row_dy = part_dy.reshape(-1, width)
    row_g = part_g.reshape(-1, 1)
    pre_gate = jnp.dot(row_x, w_gate, preferred_element_type=jnp.float32)
    pre_up = jnp.dot(row_x, w_up, preferred_element_type=jnp.float32)
    sigma = jax.nn.sigmoid(pre_gate)
    active = pre_gate * sigma
    hidden = (active * pre_up).astype(jnp.bfloat16)
    back = lax.dot_general(
        row_dy, w_down, (((1,), (1,)), ((), ())), preferred_element_type=jnp.float32
    )
    score = jnp.sum(hidden.astype(jnp.float32) * back, axis=1)
    scaled = row_dy * row_g
    d_hidden = row_g.astype(jnp.float32) * back
    d_gate = (d_hidden * pre_up * sigma * (1.0 + pre_gate * (1.0 - sigma))).astype(jnp.bfloat16)
    d_up = (d_hidden * active).astype(jnp.bfloat16)
    grad_gate = lax.dot_general(row_x, d_gate, contract, preferred_element_type=jnp.float32)
    grad_up = lax.dot_general(row_x, d_up, contract, preferred_element_type=jnp.float32)
    grad_down = lax.dot_general(hidden, scaled, contract, preferred_element_type=jnp.float32)
    scores = score.reshape(block_count, CAP)
    grad_gate, grad_up, grad_down, scores = (grad_gate, grad_up, grad_down, scores)
    summed = lax.psum(scores, "dp")
    own_scores = lax.dynamic_slice_in_dim(summed, lax.axis_index("dp") * axis_len, axis_len, 0)
    returned = lax.all_to_all(own_scores, "expert", split_axis=0, concat_axis=0, tiled=True)
    picked = returned.reshape(-1)[jnp.minimum(slots, slot_count - 1)]
    score_grad = jnp.where(valid, picked, 0.0).reshape(tok_count, top_count)
    out_gate = grad_gate.astype(jnp.bfloat16)[None]
    out_up = grad_up.astype(jnp.bfloat16)[None]
    out_down = grad_down.astype(jnp.bfloat16)[None]
    return (out_gate, out_up, out_down, score_grad)


def solution(mesh):
    placed = (
        P(("dp", "expert"), None),
        P(("dp", "expert"), None),
        P(("dp", "expert"), None),
        P(("dp", "expert"), None),
        P(),
        P("expert", None, "dp"),
        P("expert", None, "dp"),
        P("expert", "dp", None),
    )
    return jax.shard_map(
        body,
        mesh=mesh,
        in_specs=placed,
        out_specs=(
            P("expert", None, "dp"),
            P("expert", None, "dp"),
            P("expert", "dp", None),
            P(("dp", "expert"), None),
        ),
        check_vma=False,
    )
```

profile of v0, /device:TPU:0, one launch (start us, length us, event | category | flops | bytes accessed | tf_op | source)
XLA Modules:
  0.0 607.5 jit_solution(16557147332103371462)
XLA Ops:
  7.2 0.8 copy.74
  8.2 0.1 reshape.220
  8.3 0.7 select_reduce_fusion
  9.1 4.5 reduce-window.6
  13.7 0.1 copy.77
  14.1 4.3 scatter_custom_fusion
  18.4 1.2 concatenate.9
  19.7 1.0 gather_fusion
  20.7 1.2 reshape.224
  21.8 7.4 %all-to-all-start = ((bf16[16,6,3584]{2,1,0:T(8,128)(2,1)}), bf16[16,6,3584]{2,1,0:T(8,128)(2,1)S(1)}, u32[]{:S(2)}, u32[]{:S(2)}) async-start(bf16[16,6,3584]{2,1,0:T(8,128)(2,1)} %reshape.224), calls=%async_computation | async-start | bytes 1835008 | tf_op jit(solution)/shard_map/all_to_all | solution.py:57
  29.3 2.9 collective-permute-start.2
  32.2 0.1 collective-permute-start.1
  32.3 18.2 %all-to-all-done = bf16[16,6,3584]{2,1,0:T(8,128)(2,1)S(1)} async-done(((bf16[16,6,3584]{2,1,0:T(8,128)(2,1)}), bf16[16,6,3584]{2,1,0:T(8,128)(2,1)S(1)}, u32[]{:S(2)}, u32[]{:S(2)}) %all-to-all-start) | async-done | bytes 688160 | tf_op jit(solution)/shard_map/all_to_all | solution.py:57
  50.5 1.1 copy.79
  51.7 1.0 gather_fusion.2
  52.7 1.2 reshape.228
  53.8 163.4 %all-to-all-start.2 = ((bf16[16,6,3584]{2,1,0:T(8,128)(2,1)}), bf16[16,6,3584]{2,1,0:T(8,128)(2,1)S(1)}, u32[]{:S(2)}, u32[]{:S(2)}) async-start(bf16[16,6,3584]{2,1,0:T(8,128)(2,1)} %reshape.228), calls=%async_computation.2 | async-start | bytes 1835008 | tf_op jit(solution)/shard_map/all_to_all | solution.py:58
  217.3 2.9 collective-permute-start
  220.2 242.5 %all-to-all-done.2 = bf16[16,6,3584]{2,1,0:T(8,128)(2,1)S(1)} async-done(((bf16[16,6,3584]{2,1,0:T(8,128)(2,1)}), bf16[16,6,3584]{2,1,0:T(8,128)(2,1)S(1)}, u32[]{:S(2)}, u32[]{:S(2)}) %all-to-all-start.2) | async-done | bytes 688160 | tf_op jit(solution)/shard_map/all_to_all | solution.py:58
  462.7 1.1 copy.83
  463.8 0.1 copy.81
  463.9 0.1 reshape.226
  464.0 1.3 gather_fusion.1
  465.3 0.7 all_to_all.27
  466.0 6.9 %all-to-all-start.1 = ((bf16[16,1,6]{2,1,0:T(2,128)(2,1)}), bf16[16,1,6]{2,1,0:T(2,128)(2,1)S(1)}, u32[]{:S(2)}, u32[]{:S(2)}) async-start(bf16[16,1,6]{2,1,0:T(2,128)(2,1)} %all_to_all.27), calls=%async_computation.1 | async-start | bytes 16384 | tf_op jit(solution)/shard_map/all_to_all | solution.py:59
  472.9 0.6 fusion.30
  474.2 71.4 %all-to-all-done.1 = bf16[16,1,6]{2,1,0:T(2,128)(2,1)S(1)} async-done(((bf16[16,1,6]{2,1,0:T(2,128)(2,1)}), bf16[16,1,6]{2,1,0:T(2,128)(2,1)S(1)}, u32[]{:S(2)}, u32[]{:S(2)}) %all-to-all-start.1) | async-done | bytes 224 | tf_op jit(solution)/shard_map/all_to_all | solution.py:59
  545.6 4.5 all-gather
  550.2 0.1 reshape.227
  550.4 2.1 copy.80
  552.5 1.3 reshape.225
  553.8 2.1 copy.84
  555.9 0.5 reshape.229
  556.5 3.5 fusion.3
  560.0 0.4 copy-done.5
  560.4 3.2 fusion.5
  563.6 3.5 multiply_reduce_fusion
  567.1 3.2 fusion
  570.3 3.1 fusion.1
  573.5 8.2 %psum.7 = f32[32,6]{1,0:T(8,128)S(1)} all-reduce(f32[32,6]{1,0:T(8,128)S(1)} %reshape.230), channel_id=1, replica_groups=mesh['dp'=2,'expert'=16] {'dp'}, use_global_device_ids=true, to_apply=%region_7.8 | all-reduce | flops 192 | bytes 1536 | tf_op jit(solution)/shard_map/psum | solution.py:95
  581.6 0.6 constant_dynamic-slice_fusion
  582.2 3.4 all-to-all-start.3
  585.7 3.0 fusion.2
  588.7 3.3 all-to-all-done.3
  592.0 0.5 broadcast.262
  592.5 0.7 reduce.4
  593.3 6.6 %gather_fusion.3 = f32[1024]{0:T(1024)S(1)} fusion(f32[96]{0:T(128)S(1)} %reshape.231, s32[1024]{0:T(1024)S(1)} %broadcast_clamp_fusion), kind=kCustom, calls=%fused_computation.3 | custom fusion | bytes 12288 | tf_op jit(solution)/shard_map/gather | solution.py:98
  600.0 0.6 compare_select_fusion.4
  (51 shorter events, 1.2 us)
Async XLA Ops:
  20.7 30.9 %copy-start.1 = (bf16[128,3584]{1,0:T(8,128)(2,1)S(1)}, bf16[128,3584]{1,0:T(8,128)(2,1)}, u32[]{:S(2)}) copy-start(bf16[128,3584]{1,0:T(8,128)(2,1)} %param.9) | copy-start | bytes 2752516
  21.8 28.7 %all-to-all-start = ((bf16[16,6,3584]{2,1,0:T(8,128)(2,1)}), bf16[16,6,3584]{2,1,0:T(8,128)(2,1)S(1)}, u32[]{:S(2)}, u32[]{:S(2)}) async-start(bf16[16,6,3584]{2,1,0:T(8,128)(2,1)} %reshape.224), calls=%async_computation | async-start | bytes 1835008 | tf_op jit(solution)/shard_map/all_to_all | solution.py:57
  29.2 521.1 %all-gather.4.cloned.1.call-start = ((), (), s32[]{:S(2)}) async-start(), calls=%async_computation.4 | async-start | bytes 2064384 | tf_op jit(solution)/shard_map/all_gather | solution.py:70
  29.3 527.2 %collective-permute-start.2 = (bf16[1,3584,512]{2,1,0:T(8,128)(2,1)}, bf16[1,3584,512]{2,1,0:T(8,128)(2,1)}, u32[]{:S(2)}, u32[]{:S(2)}) collective-permute-start(bf16[1,3584,512]{2,1,0:T(8,128)(2,1)} %param.13), channel_id=1, source_target_pairs={{0,8},{8,0},{1,9},{9,1},{2,10},{10,2},{3,11},{11,3},{4,12},{12,4},... | collective-permute-start | bytes 11010056 | tf_op jit(solution)/shard_map/ppermute | solution.py:16
  32.2 527.8 %collective-permute-start.1 = (bf16[1,3584,512]{2,1,0:T(8,128)(2,1)}, bf16[1,3584,512]{2,1,0:T(8,128)(2,1)}, u32[]{:S(2)}, u32[]{:S(2)}) collective-permute-start(bf16[1,3584,512]{2,1,0:T(8,128)(2,1)} %param.14), channel_id=1, source_target_pairs={{0,8},{8,0},{1,9},{9,1},{2,10},{10,2},{3,11},{11,3},{4,12},{12,4},... | collective-permute-start | bytes 11010056 | tf_op jit(solution)/shard_map/ppermute | solution.py:16
  52.7 411.1 %copy-start.3 = (bf16[128,8]{0,1:T(8,128)(2,1)S(1)}, bf16[128,8]{0,1:T(8,128)(2,1)}, u32[]{:S(2)}) copy-start(bf16[128,8]{0,1:T(8,128)(2,1)} %param.11) | copy-start | bytes 6148
  52.7 420.2 %copy-start.4 = (s32[8]{0:T(128)S(1)}, s32[8]{0:T(128)}, u32[]{:S(2)}) copy-start(s32[8]{0:T(128)} %param.12) | copy-start | bytes 100
  53.8 408.9 %all-to-all-start.2 = ((bf16[16,6,3584]{2,1,0:T(8,128)(2,1)}), bf16[16,6,3584]{2,1,0:T(8,128)(2,1)S(1)}, u32[]{:S(2)}, u32[]{:S(2)}) async-start(bf16[16,6,3584]{2,1,0:T(8,128)(2,1)} %reshape.228), calls=%async_computation.2 | async-start | bytes 1835008 | tf_op jit(solution)/shard_map/all_to_all | solution.py:58
  217.2 336.6 %all-gather.6.cloned.1.call-start = ((), (), s32[]{:S(2)}) async-start(), calls=%async_computation.5 | async-start | bytes 2064384 | tf_op jit(solution)/shard_map/all_gather | solution.py:71
  217.3 346.3 %collective-permute-start = (bf16[1,512,3584]{2,1,0:T(8,128)(2,1)}, bf16[1,512,3584]{2,1,0:T(8,128)(2,1)}, u32[]{:S(2)}, u32[]{:S(2)}) collective-permute-start(bf16[1,512,3584]{2,1,0:T(8,128)(2,1)} %param.15), channel_id=1, source_target_pairs={{0,8},{8,0},{1,9},{9,1},{2,10},{10,2},{3,11},{11,3},{4,12},{12,4},... | collective-permute-start | bytes 11010056 | tf_op jit(solution)/shard_map/ppermute | solution.py:16
  466.0 79.6 %all-to-all-start.1 = ((bf16[16,1,6]{2,1,0:T(2,128)(2,1)}), bf16[16,1,6]{2,1,0:T(2,128)(2,1)S(1)}, u32[]{:S(2)}, u32[]{:S(2)}) async-start(bf16[16,1,6]{2,1,0:T(2,128)(2,1)} %all_to_all.27), calls=%async_computation.1 | async-start | bytes 16384 | tf_op jit(solution)/shard_map/all_to_all | solution.py:59
  556.4 3.6 copy-start
  556.4 4.0 copy-start.5
  560.0 3.6 copy-start.6
  582.2 9.8 %all-to-all-start.3 = ((f32[16,1,6]{2,1,0:T(1,128)}), f32[16,1,6]{2,1,0:T(1,128)S(1)}, u32[]{:S(2)}, u32[]{:S(2)}) async-start(f32[16,1,6]{2,1,0:T(1,128)} %bitcast.13), calls=%async_computation.3 | async-start | bytes 16384 | tf_op jit(solution)/shard_map/all_to_all | solution.py:97
  585.6 14.4 %copy-start.2 = (s32[128,8]{0,1:T(8,128)S(1)}, s32[128,8]{0,1:T(8,128)}, u32[]{:S(2)}) copy-start(s32[128,8]{0,1:T(8,128)} %param.10) | copy-start | bytes 12292
Sparse Core Ops, SparseCore 0:
  51.7 183.7 all-gather.3
  463.9 27.2 all-gather.5
where the time goes:
time: 608 us; the launch traced here: 607 us
  waiting for transfers between devices  336 us (55%)
  starting transfers between devices  187 us (31%)
  local copies, waits for them, and re-layouts  30.1 us (5%)
  matrix products  19.5 us (3%)
  between operations  15.1 us (2%)
  blocking collectives  12.7 us (2%)
  other arithmetic  7.5 us (1%)
    all_to_all x1, waiting for transfers between devices, body(): lax.all_to_all(send_dy, 'expert', split_axis=0, concat_axis=0, tiled=True)  243 us
    all_to_all x1, starting transfers between devices, body(): lax.all_to_all(send_dy, 'expert', split_axis=0, concat_axis=0, tiled=True)  163 us
    all_to_all x1, waiting for transfers between devices, body(): lax.all_to_all(send_g, 'expert', split_axis=0, concat_axis=0, tiled=True)  71.4 us
    all_to_all x1, waiting for transfers between devices, body(): lax.all_to_all(send_x, 'expert', split_axis=0, concat_axis=0, tiled=True)  18.2 us
  transfers between devices with their start and end apart: 9, of which 4 were waited for; matrix products, arithmetic and copies ran while one was open for 4% of the time, Pallas kernels for 0%

commit v1 on v0

v1 whole, which is shorter than its diff:
```python
import functools
import math

import jax
import jax.numpy as jnp
from jax import lax
from jax.experimental import pallas as pl
from jax.experimental.pallas import tpu as pltpu
from jax.sharding import PartitionSpec as P

CAP = 6
CUTS = 4
SUB = CAP * CUTS
BLOCK = 2 * SUB
LANES = 128
AHEAD = 2
MIB = 1024 * 1024


def params(*arrays):
    held = sum(math.prod(shape) * size for shape, size in arrays)
    return pltpu.CompilerParams(vmem_limit_bytes=min(56 * MIB, held + 6 * MIB))


def pack_kernel(half, place_ref, ids_ref, gates_ref, tokens_ref, cot_ref, *refs):
    wire0_ref, wire1_ref, mine_ref, theirs_ref, pos_ref, rows_ref, sems = refs
    top, count = ids_ref.shape
    quarter = tokens_ref.shape[1] // CUTS
    experts = 2 * half
    copies = []
    for kind, source in enumerate((tokens_ref, cot_ref)):
        for q in range(CUTS):
            n = kind * CUTS + q
            copies.append(
                pltpu.make_async_copy(
                    source.at[:, pl.ds(q * quarter, quarter)],
                    rows_ref.at[pl.ds(n * count, count), :],
                    sems.at[n],
                )
            )
            copies[-1].start()
    ids = ids_ref[...]
    gates = gates_ref[...].astype(jnp.float32)
    expert = lax.broadcasted_iota(jnp.int32, (experts, count), 0)
    named = jnp.zeros((experts, count), jnp.float32)
    gate_of = jnp.zeros((experts, count), jnp.float32)
    for k in range(top):
        hit = ids[k : k + 1, :] == expert
        named = named + jnp.where(hit, 1.0, 0.0)
        gate_of = gate_of + jnp.where(hit, gates[k : k + 1, :], 0.0)
    earlier = lax.broadcasted_iota(jnp.int32, (count, count), 0) < lax.broadcasted_iota(
        jnp.int32, (count, count), 1
    )
    rank = jnp.dot(
        named.astype(jnp.bfloat16),
        jnp.where(earlier, 1.0, 0.0).astype(jnp.bfloat16),
        preferred_element_type=jnp.float32,
    )
    place = (expert * CAP + 1).astype(jnp.float32) + rank
    line = lax.broadcasted_iota(jnp.int32, (top, count), 0)
    pos = jnp.zeros((top, count), jnp.float32)
    for k in range(top):
        found = jnp.sum(jnp.where(ids[k : k + 1, :] == expert, place, 0.0), axis=0, keepdims=True)
        pos = jnp.where(line == k, found, pos)
    pos_ref[...] = pos.astype(jnp.int32) - 1
    per_token = jnp.concatenate([named, rank, gate_of], axis=1).astype(jnp.bfloat16)
    rows = half * BLOCK
    sub = lax.broadcasted_iota(jnp.int32, (rows, 1), 0)
    kind_cut = (sub % BLOCK) // CAP
    nth = (sub % CAP).astype(jnp.float32)
    low, side = place_ref[0] % half, place_ref[0] // half
    owner = lax.broadcasted_iota(jnp.int32, (rows, experts), 1)
    for rel, wire_ref in ((0, wire0_ref), (1, wire1_ref)):
        wanted = sub // BLOCK + half * (1 - side if rel else side)
        spread = jnp.where(owner == wanted, 1.0, 0.0).astype(jnp.bfloat16)
        seen = jnp.dot(spread, per_token, preferred_element_type=jnp.float32)
        chosen = (seen[:, :count] > 0.5) & (seen[:, count : 2 * count] == nth)
        pick_x = jnp.where(chosen, 1.0, 0.0)
        pick_s = jnp.where(chosen, seen[:, 2 * count :], 0.0)
        picks = [jnp.where(kind_cut == q, pick_x, 0.0) for q in range(CUTS)]
        picks += [jnp.where(kind_cut == CUTS + q, pick_s, 0.0) for q in range(CUTS)]
        picks = jnp.concatenate(picks, axis=1).astype(jnp.bfloat16)
        if rel == 0:
            for copy in copies:
                copy.wait()
        wire_ref[...] = jnp.dot(
            picks, rows_ref[...], preferred_element_type=jnp.float32
        ).astype(jnp.bfloat16)
    for core, turned_ref in enumerate((mine_ref, theirs_ref)):
        for c in range(half // 2):
            source = pl.multiple_of(jnp.bitwise_xor(low, 2 * c + core) * BLOCK, BLOCK)
            turned_ref[c * BLOCK : (c + 1) * BLOCK, :] = wire1_ref[pl.ds(source, BLOCK), :]


def pack(place, ids, gates, tokens, cotangent, half):
    count, width = tokens.shape
    quarter = width // CUTS
    vmem = pl.BlockSpec(memory_space=pltpu.VMEM)
    hbm = pl.BlockSpec(memory_space=pltpu.HBM)
    wire = jax.ShapeDtypeStruct((half * BLOCK, quarter), jnp.bfloat16)
    halved = jax.ShapeDtypeStruct((half * BLOCK // 2, quarter), jnp.bfloat16)
    return pl.pallas_call(
        functools.partial(pack_kernel, half),
        out_shape=(wire, wire, halved, halved, jax.ShapeDtypeStruct(ids.shape, jnp.int32)),
        in_specs=[pl.BlockSpec(memory_space=pltpu.SMEM), vmem, vmem, hbm, hbm],
        out_specs=(vmem,) * 5,
        scratch_shapes=[
            pltpu.VMEM((2 * CUTS * count, quarter), jnp.bfloat16),
            pltpu.SemaphoreType.DMA((2 * CUTS,)),
        ],
        compiler_params=pltpu.CompilerParams(vmem_limit_bytes=56 * MIB),
        name="pack",
    )(place, ids, gates, tokens, cotangent)


def order_matrix(half, turn):
    rows = half * BLOCK
    out = lax.broadcasted_iota(jnp.int32, (rows, 1), 0)
    sub = lax.broadcasted_iota(jnp.int32, (rows, rows), 1)
    group, inner = out // (half * CAP), out % (half * CAP)
    wanted = jnp.bitwise_xor(inner // CAP, turn) * BLOCK + group * CAP + inner % CAP
    return jnp.where(wanted == sub, 1.0, 0.0).astype(jnp.bfloat16)


def home_kernel(half, wires, *refs):
    wire_refs = refs[:wires]
    sources = refs[wires : wires + 3]
    acts_ref, score_ref, x_ref, s_ref, gate_ref, up_ref, down_ref, sems = refs[wires + 3 :]
    rows = half * CAP
    quarter = wire_refs[0].shape[1]
    hidden_width = gate_ref.shape[1]
    copies = []
    for q in range(CUTS):
        columns = pl.ds(q * quarter, quarter)
        for n, (source, target) in enumerate(zip(sources, (gate_ref, up_ref, down_ref))):
            place = (slice(None), columns) if n == 2 else (columns, slice(None))
            copies.append(
                pltpu.make_async_copy(source.at[place], target.at[place], sems.at[3 * q + n])
            )
    for copy in copies[: 3 * AHEAD]:
        copy.start()
    order = order_matrix(half, 0)
    for w in range(wires):
        sorted_rows = jnp.dot(
            order, wire_refs[w][...], preferred_element_type=jnp.float32
        ).astype(jnp.bfloat16)
        for q in range(CUTS):
            place = (q, pl.ds(w * rows, rows))
            x_ref[place] = sorted_rows[q * rows : (q + 1) * rows]
            s_ref[place] = sorted_rows[(CUTS + q) * rows : (CUTS + q + 1) * rows]
    total = wires * rows
    pre_gate = pre_up = d_hidden = jnp.zeros((total, hidden_width), jnp.float32)
    for q in range(CUTS):
        columns = pl.ds(q * quarter, quarter)
        for copy in copies[3 * q : 3 * q + 3]:
            copy.wait()
        for copy in copies[3 * (q + AHEAD) : 3 * (q + AHEAD) + 3]:
            copy.start()
        pre_gate += jnp.dot(x_ref[q], gate_ref[columns, :], preferred_element_type=jnp.float32)
        pre_up += jnp.dot(x_ref[q], up_ref[columns, :], preferred_element_type=jnp.float32)
        d_hidden += lax.dot_general(
            s_ref[q],
            down_ref[:, columns],
            (((1,), (1,)), ((), ())),
            preferred_element_type=jnp.float32,
        )
    sigma = 1.0 / (1.0 + jnp.exp(-pre_gate))
    active = pre_gate * sigma
    hidden = (active * pre_up).astype(jnp.bfloat16)
    d_gate = d_hidden * pre_up * sigma * (1.0 + pre_gate * (1.0 - sigma))
    acts_ref[:, :hidden_width] = hidden
    acts_ref[:, hidden_width : 2 * hidden_width] = d_gate.astype(jnp.bfloat16)
    acts_ref[:, 2 * hidden_width :] = (d_hidden * active).astype(jnp.bfloat16)
    score = jnp.sum(hidden.astype(jnp.float32) * d_hidden, axis=1, keepdims=True)
    row = lax.broadcasted_iota(jnp.int32, (total, 1), 0) % CAP
    lane = lax.broadcasted_iota(jnp.int32, (total, LANES), 1)
    spread = jnp.where(row == lane, score, 0.0)
    line = lax.broadcasted_iota(jnp.int32, (wires * half, 1), 0)
    group = (line % wires) * rows + (line // wires) * CAP
    member = lax.broadcasted_iota(jnp.int32, (wires * half, total), 1)
    score_ref[...] = jnp.dot(
        jnp.where((member >= group) & (member < group + CAP), 1.0, 0.0),
        spread,
        precision=lax.Precision.HIGHEST,
        preferred_element_type=jnp.float32,
    )


def home(wires, w_gate, w_up, w_down, half):
    width, hidden_width = w_gate.shape
    count = len(wires)
    rows = count * half * CAP
    vmem = pl.BlockSpec(memory_space=pltpu.VMEM)
    hbm = pl.BlockSpec(memory_space=pltpu.HBM)
    scratch = pltpu.VMEM((CUTS, rows, width // CUTS), jnp.bfloat16)
    return pl.pallas_call(
        functools.partial(home_kernel, half, count),
        out_shape=(
            jax.ShapeDtypeStruct((rows, 3 * hidden_width), jnp.bfloat16),
            jax.ShapeDtypeStruct((count * half, LANES), jnp.float32),
        ),
        in_specs=[vmem] * count + [hbm] * 3,
        out_specs=(vmem, vmem),
        scratch_shapes=[scratch, scratch]
        + [pltpu.VMEM(w.shape, jnp.bfloat16) for w in (w_gate, w_up, w_down)]
        + [pltpu.SemaphoreType.DMA((3 * CUTS,))],
        compiler_params=pltpu.CompilerParams(vmem_limit_bytes=56 * MIB),
        name="home",
    )(*wires, w_gate, w_up, w_down)


def sort_kernel(half, wires, turns, slot_ref, flag_ref, *refs):
    own_wires, slot_wires = refs[:wires], refs[wires : 2 * wires]
    x_ref, s_ref, wire_ref, sems = refs[2 * wires :]
    rows = half * CAP
    taken = flag_ref[0] == 1

    def fetch(w, source):
        pltpu.make_async_copy(source, wire_ref.at[w], sems.at[w]).start()

    for w in range(wires):
        pl.when(taken)(functools.partial(fetch, w, slot_wires[w]))
        pl.when(jnp.logical_not(taken))(functools.partial(fetch, w, own_wires[w]))
    order = order_matrix(half, jnp.where(taken, slot_ref[0] % half, 0) if turns else 0)
    for w in range(wires):
        pltpu.make_async_copy(own_wires[w], wire_ref.at[w], sems.at[w]).wait()
        sorted_rows = jnp.dot(order, wire_ref[w], preferred_element_type=jnp.float32).astype(
            jnp.bfloat16
        )
        for q in range(CUTS):
            x_ref[q, pl.ds(w * rows, rows), :] = sorted_rows[q * rows : (q + 1) * rows]
            s_ref[q, pl.ds(w * rows, rows), :] = sorted_rows[
                (CUTS + q) * rows : (CUTS + q + 1) * rows
            ]


def sort_rows(slot, flag, own_wires, slot_wires, turns, half):
    count = len(own_wires)
    quarter = own_wires[0].shape[1]
    rows = count * half * CAP
    vmem = pl.BlockSpec(memory_space=pltpu.VMEM)
    hbm = pl.BlockSpec(memory_space=pltpu.HBM)
    smem = pl.BlockSpec(memory_space=pltpu.SMEM)
    shape = jax.ShapeDtypeStruct((CUTS, rows, quarter), jnp.bfloat16)
    return pl.pallas_call(
        functools.partial(sort_kernel, half, count, turns),
        out_shape=(shape, shape),
        in_specs=[smem, smem] + [hbm] * (2 * count),
        out_specs=(vmem, vmem),
        scratch_shapes=[
            pltpu.VMEM((count, half * BLOCK, quarter), jnp.bfloat16),
            pltpu.SemaphoreType.DMA((count,)),
        ],
        compiler_params=params(((rows, CUTS * quarter), 2 * 2), (own_wires[0].shape, 2 * count + 8)),
        name="sort_rows",
    )(slot, flag, *own_wires, *slot_wires)


def grads_kernel(parts, flag_ref, *refs):
    own_refs, other_refs = refs[:parts], refs[parts : 2 * parts]
    x_refs, s_refs = refs[2 * parts : 3 * parts], refs[3 * parts : 4 * parts]
    gate_ref, up_ref, down_ref, acts_ref = refs[4 * parts :]
    rows = own_refs[0].shape[0]
    hidden_width = gate_ref.shape[1]

    @pl.when(pl.program_id(0) == 0)
    def _():
        taken = flag_ref[0] == 1
        for p in range(parts):
            acts_ref[pl.ds(p * rows, rows), :] = jnp.where(
                taken, other_refs[p][...], own_refs[p][...]
            )

    contract = (((0,), (0,)), ((), ()))
    x = jnp.concatenate([ref[0] for ref in x_refs], axis=0)
    s = jnp.concatenate([ref[0] for ref in s_refs], axis=0)
    out = lax.dot_general(
        x, acts_ref[:, hidden_width:], contract, preferred_element_type=jnp.float32
    )
    gate_ref[...] = out[:, :hidden_width].astype(jnp.bfloat16)
    up_ref[...] = out[:, hidden_width:].astype(jnp.bfloat16)
    down_ref[...] = lax.dot_general(
        acts_ref[:, :hidden_width], s, contract, preferred_element_type=jnp.float32
    ).astype(jnp.bfloat16)


def grads(flag, own, other, x_parts, s_parts):
    count = len(own)
    cuts, rows, quarter = x_parts[0].shape
    width = cuts * quarter
    triple = own[0].shape[1]
    hidden_width = triple // 3
    vmem = pl.BlockSpec(memory_space=pltpu.VMEM)
    part = pl.BlockSpec((1, rows, quarter), lambda q: (q, 0, 0))
    return pl.pallas_call(
        functools.partial(grads_kernel, count),
        grid=(cuts,),
        out_shape=(
            jax.ShapeDtypeStruct((width, hidden_width), jnp.bfloat16),
            jax.ShapeDtypeStruct((width, hidden_width), jnp.bfloat16),
            jax.ShapeDtypeStruct((hidden_width, width), jnp.bfloat16),
        ),
        in_specs=[pl.BlockSpec(memory_space=pltpu.SMEM)] + [vmem] * (2 * count) + [part] * (2 * count),
        out_specs=(
            pl.BlockSpec((quarter, hidden_width), lambda q: (q, 0)),
            pl.BlockSpec((quarter, hidden_width), lambda q: (q, 0)),
            pl.BlockSpec((hidden_width, quarter), lambda q: (0, q)),
        ),
        scratch_shapes=[pltpu.VMEM((count * rows, triple), jnp.bfloat16)],
        compiler_params=params(
            ((count * rows, triple), 3 * 2),
            ((count * rows, quarter), 2 * 3 * 2),
            ((quarter, hidden_width), 3 * (2 * 2 + 4)),
        ),
        name="grads",
    )(flag, *own, *other, *x_parts, *s_parts)


def body(tokens, cotangent, expert_ids, gates, swap_flags, gate_w, up_w, down_w):
    axis_len = lax.axis_size("expert")
    planes = lax.axis_size("dp")
    half = axis_len // 2
    own_slot = lax.axis_index("expert")
    side, low = own_slot // half, own_slot % half
    quarter = tokens.shape[1] // CUTS
    groups = [list(range(half)), list(range(half, axis_len))]
    slot = own_slot.reshape(1)
    flag = lax.dynamic_slice_in_dim(swap_flags, low, 1, 0)

    def exchange(wire, name):
        with jax.named_scope("t_" + name):
            blocks = wire.reshape(half, BLOCK, quarter)
            moved = lax.all_to_all(
                blocks, "expert", split_axis=0, concat_axis=0, tiled=True, axis_index_groups=groups
            )
            return moved.reshape(half * BLOCK, quarter)

    def flip(block, by, name):
        with jax.named_scope("t_" + name):
            return lax.ppermute(block, "expert", [(i, i ^ by) for i in range(axis_len)])

    def across(block, name):
        return flip(block, half, name)

    def turned_exchange(mine, theirs, name, behind):
        pieces = []
        for c in range(half // 2):
            part = slice(c * BLOCK, (c + 1) * BLOCK)
            piece = jnp.concatenate([mine[part], theirs[part]], axis=0)
            pieces.append(flip(piece, 2 * c, name + str(c)) if c else piece)
        pieces = lax.optimization_barrier(tuple(pieces) + behind)[: half // 2]
        return jnp.concatenate(pieces, axis=0)

    def all_planes(wire, name):
        with jax.named_scope("t_" + name):
            return [wire] + [
                lax.ppermute(wire, "dp", [(i, (i + by) % planes) for i in range(planes)])
                for by in range(1, planes)
            ]

    def after(value, *others):
        return lax.optimization_barrier((value,) + others)[0]

    wire0, wire1, mine, theirs, pos = pack(
        slot, expert_ids.T, gates.T, tokens, cotangent, half
    )
    moved = across(wire1, "M")
    theirs = flip(theirs, 1, "A1c")
    home0 = exchange(wire0, "A0")
    homes0 = all_planes(home0, "xR0")
    slot1 = turned_exchange(mine, theirs, "A1", ())
    home1 = exchange(after(moved, slot1, *homes0[1:]), "A2")
    crossed = across(after(home0, moved, *homes0[1:]), "O")
    slots1 = all_planes(slot1, "xR1")
    homes1 = all_planes(home1, "xRM")
    homes1[0] = after(homes1[0], crossed, *slots1[1:])
    acts0, score0 = home(homes0, gate_w[0], up_w[0], down_w[0], half)
    slots0 = all_planes(after(crossed, acts0), "xO")
    acts1, score1 = home(homes1, gate_w[0], up_w[0], down_w[0], half)
    own = [acts0, acts1]
    other = [across(after(acts0, crossed), "acts0"), across(acts1, "acts1")]
    rows0 = sort_rows(slot, flag, homes0, slots0, False, half)
    rows1 = sort_rows(slot, flag, homes1, slots1, True, half)

    near = score0.reshape(half, planes, LANES)
    far = score1.reshape(half, planes, LANES)
    near, far = lax.optimization_barrier((near, far) + ())[:2]
    back = jnp.concatenate([jnp.where(side == 0, near, far), jnp.where(side == 0, far, near)])
    returned = lax.all_to_all(back, "expert", split_axis=0, concat_axis=0, tiled=True)
    returned = after(returned, rows0[0], rows1[0])
    sums = [returned[:, 0]]
    for by in range(1, planes):
        sums.append(
            lax.ppermute(returned[:, by], "dp", [(i, (i - by) % planes) for i in range(planes)])
        )

    out_gate, out_up, out_down = grads(
        flag, own, other, [rows0[0], rows1[0]], [rows0[1], rows1[1]]
    )
    total = sum(lax.optimization_barrier((*sums, out_down))[:-1])
    values = total[:, :CAP].reshape(-1)
    match = pos[:, :, None] == jnp.arange(axis_len * CAP, dtype=jnp.int32)[None, None, :]
    picked = jnp.sum(jnp.where(match, values[None, None, :], 0.0), axis=2)
    score_grad = (picked / gates.T.astype(jnp.float32)).T

    return (out_gate[None], out_up[None], out_down[None], score_grad)


def solution(mesh):
    placed = (
        P(("dp", "expert"), None),
        P(("dp", "expert"), None),
        P(("dp", "expert"), None),
        P(("dp", "expert"), None),
        P(),
        P("expert", None, "dp"),
        P("expert", None, "dp"),
        P("expert", "dp", None),
    )
    return jax.shard_map(
        body,
        mesh=mesh,
        in_specs=placed,
        out_specs=(
            P("expert", None, "dp"),
            P("expert", None, "dp"),
            P("expert", "dp", None),
            P(("dp", "expert"), None),
        ),
        check_vma=False,
    )
```

time: 608 us -> 126 us (0.21)
  waiting for transfers between devices: 336 us -> 52.1 us
  starting transfers between devices: 187 us -> 30.2 us
  Pallas kernels: 0 us -> 33.1 us
  local copies, waits for them, and re-layouts: 30.1 us -> 6.91 us
  matrix products: 19.5 us -> 0 us
  between operations: 15.1 us -> 0.92 us
  blocking collectives: 12.7 us -> 0 us
    all_to_all x4 -> x3, waiting for transfers between devices: 335 us -> 30.3 us  [the longest x2 27.3 us: exchange(): lax.all_to_all(blocks, 'expert', split_axis=0, concat_axis=0, tiled=True,...]
    all_to_all x4 -> x3, starting transfers between devices: 181 us -> 13.2 us  [the longest x2 8.82 us: exchange(): lax.all_to_all(blocks, 'expert', split_axis=0, concat_axis=0, tiled=True,...]
    pallas_call x0 -> x6, Pallas kernels: none -> 33.1 us  [the longest x2 15 us: home(): pl.pallas_call(functools.partial(home_kernel, half, count), out_shape=(ja...]
    ppermute x3 -> x13, waiting for transfers between devices: 0.01 us -> 21.8 us  [the longest x8 19.5 us: flip(): return lax.ppermute(block, 'expert', [(i, i ^ by) for i in range(axis_len)])]
    dot_general x6 -> x0, matrix products: 19.5 us -> none  [the longest x1 3.5 us: body(): pre_gate = jnp.dot(row_x, w_gate, preferred_element_type=jnp.float32)]
    ppermute x3 -> x13, starting transfers between devices: 5.88 us -> 17 us  [the longest x8 10.4 us: flip(): return lax.ppermute(block, 'expert', [(i, i ^ by) for i in range(axis_len)])]
    gather x6 -> x0, local copies, waits for them, and re-layouts: 9.91 us -> none  [the longest x3 6.7 us: body(): picked = returned.reshape(-1)[jnp.minimum(slots, slot_count - 1)]]
    psum x1 -> x0, blocking collectives: 8.15 us -> none  [body(): summed = lax.psum(scores, 'dp')]
  transfers between devices with their start and end apart: 9 -> 16, of which waited for: 4 -> 8; matrix products, arithmetic and copies ran while one was open for 4% -> 3% of each run, Pallas kernels for 0% -> 22%
where the time goes in v1:
time: 126 us; the launch traced here: 125 us
  waiting for transfers between devices  52.1 us (41%)
  Pallas kernels  33.1 us (26%)
  starting transfers between devices  30.2 us (24%)
  local copies, waits for them, and re-layouts  6.91 us (5%)
  other arithmetic  2.1 us (2%)
    all_to_all x2, waiting for transfers between devices, exchange(): lax.all_to_all(blocks, 'expert', split_axis=0, concat_axis=0, tiled=True,...  27.3 us
    ppermute x8, waiting for transfers between devices, flip(): return lax.ppermute(block, 'expert', [(i, i ^ by) for i in range(axis_len)])  19.5 us
    pallas_call x2, Pallas kernels, home(): pl.pallas_call(functools.partial(home_kernel, half, count), out_shape=(ja...  15 us
    ppermute x8, starting transfers between devices, flip(): return lax.ppermute(block, 'expert', [(i, i ^ by) for i in range(axis_len)])  10.4 us
    all_to_all x2, starting transfers between devices, exchange(): lax.all_to_all(blocks, 'expert', split_axis=0, concat_axis=0, tiled=True,...  8.82 us
    pallas_call x1, Pallas kernels, grads(): pl.pallas_call(functools.partial(grads_kernel, count), grid=(cuts,), out_...  7.16 us
    ppermute x4, starting transfers between devices, all_planes(): lax.ppermute(wire, 'dp', [(i, (i + by) % planes) for i in range(planes)])  5.96 us
    pallas_call x2, Pallas kernels, sort_rows(): pl.pallas_call(functools.partial(sort_kernel, half, count, turns), out_sh...  5.62 us
  transfers between devices with their start and end apart: 16, of which 8 were waited for; matrix products, arithmetic and copies ran while one was open for 3% of the time, Pallas kernels for 22%

profile of v1, /device:TPU:0, one launch (start us, length us, event | category | flops | bytes accessed | tf_op | source)
XLA Modules:
  0.0 125.4 jit_solution(6953749740936846186)
XLA Ops:
  0.6 5.4 %pack.1 = (bf16[384,896]{1,0:T(8,128)(2,1)}, bf16[384,896]{1,0:T(8,128)(2,1)}, bf16[192,896]{1,0:T(8,128)(2,1)}, bf16[192,896]{1,0:T(8,128)(2,1)}, s32[8,128]{1,0:T(8,128)}) custom-call(s32[1]{0:T(128)} %bitcast.place_ref.slot_ref, s32[8,128]{1,0:T(8,128)} %bitcast.44, bf16[8,128]{1,0:T(8,128)(2,1)} %bitcast.40, bf16[128,3584]{1,0:T(8,128)(2,1)} %tokens_ref.1, ...), custom_call_target="tpu_custom_call" | custom-call | tf_op jit(solution)/shard_map/pack/pallas_call | solution.py:102
  6.0 5.3 %all-to-all-start = ((bf16[8,48,896]{2,1,0:T(8,128)(2,1)}), bf16[8,48,896]{2,1,0:T(8,128)(2,1)S(1)}, u32[]{:S(2)}, u32[]{:S(2)}) async-start(bf16[8,48,896]{2,1,0:T(8,128)(2,1)} %bitcast.37), calls=%async_computation | async-start | bytes 1376256 | tf_op jit(solution)/shard_map/t_A0/all_to_all | solution.py:333
  11.3 0.5 collective-permute-start.2
  11.8 2.6 %collective-permute-start.1 = (bf16[384,896]{1,0:T(8,128)(2,1)}, bf16[384,896]{1,0:T(8,128)(2,1)}, u32[]{:S(2)}, u32[]{:S(2)}) collective-permute-start(bf16[384,896]{1,0:T(8,128)(2,1)} %get-tuple-element.36), channel_id=1, source_target_pairs={{0,8},{1,9},{2,10},{3,11},{4,12},{5,13},{6,14},{7,15},{8,0},{9,1},... | collective-permute-start | bytes 2064392 | tf_op jit(solution)/shard_map/t_M/ppermute | solution.py:340
  14.4 1.0 fusion
  15.5 1.7 %collective-permute-start.3 = (bf16[96,896]{1,0:T(8,128)(2,1)S(1)}, bf16[96,896]{1,0:T(8,128)(2,1)S(1)}, u32[]{:S(2)}, u32[]{:S(2)}) collective-permute-start(bf16[96,896]{1,0:T(8,128)(2,1)S(1)} %pad_maximum_fusion.1), channel_id=1, source_target_pairs={{0,2},{1,3},{2,0},{3,1},{4,6},{5,7},{6,4},{7,5},{8,10},{9,11},{10,... | collective-permute-start | bytes 516104 | tf_op jit(solution)/shard_map/t_A11/ppermute | solution.py:340
  17.2 1.5 %collective-permute-start.4 = (bf16[96,896]{1,0:T(8,128)(2,1)S(1)}, bf16[96,896]{1,0:T(8,128)(2,1)S(1)}, u32[]{:S(2)}, u32[]{:S(2)}) collective-permute-start(bf16[96,896]{1,0:T(8,128)(2,1)S(1)} %pad_maximum_fusion.2), channel_id=1, source_target_pairs={{0,4},{1,5},{2,6},{3,7},{4,0},{5,1},{6,2},{7,3},{8,12},{9,13},{10,... | collective-permute-start | bytes 516104 | tf_op jit(solution)/shard_map/t_A12/ppermute | solution.py:340
  18.8 12.0 %all-to-all-done = bf16[8,48,896]{2,1,0:T(8,128)(2,1)S(1)} async-done(((bf16[8,48,896]{2,1,0:T(8,128)(2,1)}), bf16[8,48,896]{2,1,0:T(8,128)(2,1)S(1)}, u32[]{:S(2)}, u32[]{:S(2)}) %all-to-all-start) | async-done | bytes 688160 | tf_op jit(solution)/shard_map/t_A0/all_to_all | solution.py:333
  30.8 1.5 %collective-permute-start = (bf16[384,896]{1,0:T(8,128)(2,1)S(1)}, bf16[384,896]{1,0:T(8,128)(2,1)S(1)}, u32[]{:S(2)}, u32[]{:S(2)}) collective-permute-start(bf16[384,896]{1,0:T(8,128)(2,1)S(1)} %bitcast.24), channel_id=1, source_target_pairs={{0,16},{16,0},{1,17},{17,1},{2,18},{18,2},{3,19},{19,3},{4,20},{20... | collective-permute-start | bytes 2064392 | tf_op jit(solution)/shard_map/t_xR0/ppermute | solution.py:357
  32.3 0.1 collective-permute-start.5
  32.4 0.0 collective-permute-done.3
  32.4 6.0 %collective-permute-done.4 = bf16[96,896]{1,0:T(8,128)(2,1)S(1)} collective-permute-done((bf16[96,896]{1,0:T(8,128)(2,1)S(1)}, bf16[96,896]{1,0:T(8,128)(2,1)S(1)}, u32[]{:S(2)}, u32[]{:S(2)}) %collective-permute-start.4) | collective-permute-done | bytes 172064 | tf_op jit(solution)/shard_map/t_A12/ppermute | solution.py:340
  38.4 3.5 %collective-permute-done.5 = bf16[96,896]{1,0:T(8,128)(2,1)S(1)} collective-permute-done((bf16[96,896]{1,0:T(8,128)(2,1)S(1)}, bf16[96,896]{1,0:T(8,128)(2,1)S(1)}, u32[]{:S(2)}, u32[]{:S(2)}) %collective-permute-start.5) | collective-permute-done | bytes 172064 | tf_op jit(solution)/shard_map/t_A13/ppermute | solution.py:340
  42.1 3.1 %collective-permute-done.1 = bf16[384,896]{1,0:T(8,128)(2,1)} collective-permute-done((bf16[384,896]{1,0:T(8,128)(2,1)}, bf16[384,896]{1,0:T(8,128)(2,1)}, u32[]{:S(2)}, u32[]{:S(2)}) %collective-permute-start.1) | collective-permute-done | bytes 688160 | tf_op jit(solution)/shard_map/t_M/ppermute | solution.py:340
  45.1 2.3 %collective-permute-done.refs_1_ = bf16[384,896]{1,0:T(8,128)(2,1)S(1)} collective-permute-done((bf16[384,896]{1,0:T(8,128)(2,1)S(1)}, bf16[384,896]{1,0:T(8,128)(2,1)S(1)}, u32[]{:S(2)}, u32[]{:S(2)}) %collective-permute-start) | collective-permute-done | bytes 688160 | tf_op jit(solution)/shard_map/t_xR0/ppermute | solution.py:357
  47.4 3.5 %all-to-all-start.1 = ((bf16[8,48,896]{2,1,0:T(8,128)(2,1)}), bf16[8,48,896]{2,1,0:T(8,128)(2,1)S(1)}, u32[]{:S(2)}, u32[]{:S(2)}) async-start(bf16[8,48,896]{2,1,0:T(8,128)(2,1)} %bitcast.8), calls=%async_computation.1 | async-start | bytes 1376256 | tf_op jit(solution)/shard_map/t_A2/all_to_all | solution.py:333
  51.0 0.9 collective-permute-start.6
  51.9 1.5 %collective-permute-start.7 = (bf16[384,896]{1,0:T(8,128)(2,1)S(1)}, bf16[384,896]{1,0:T(8,128)(2,1)}, u32[]{:S(2)}, u32[]{:S(2)}) collective-permute-start(bf16[384,896]{1,0:T(8,128)(2,1)S(1)} %constant_dynamic-update-slice_fusion.refs_2_), channel_id=1, source_target_pairs={{0,16},{16,0},{1,17},{17,1},{2,18},{18,2},{3,19},{19,3},{4,20},{20... | collective-permute-start | bytes 2064392 | tf_op jit(solution)/shard_map/t_xR1/ppermute | solution.py:357
  53.4 15.2 %all-to-all-done.1 = bf16[8,48,896]{2,1,0:T(8,128)(2,1)S(1)} async-done(((bf16[8,48,896]{2,1,0:T(8,128)(2,1)}), bf16[8,48,896]{2,1,0:T(8,128)(2,1)S(1)}, u32[]{:S(2)}, u32[]{:S(2)}) %all-to-all-start.1) | async-done | bytes 688160 | tf_op jit(solution)/shard_map/t_A2/all_to_all | solution.py:333
  68.6 1.5 %collective-permute-start.8 = (bf16[384,896]{1,0:T(8,128)(2,1)S(1)}, bf16[384,896]{1,0:T(8,128)(2,1)S(1)}, u32[]{:S(2)}, u32[]{:S(2)}) collective-permute-start(bf16[384,896]{1,0:T(8,128)(2,1)S(1)} %bitcast.28), channel_id=1, source_target_pairs={{0,16},{16,0},{1,17},{17,1},{2,18},{18,2},{3,19},{19,3},{4,20},{20... | collective-permute-start | bytes 2064392 | tf_op jit(solution)/shard_map/t_xRM/ppermute | solution.py:357
  70.1 7.5 %home.2 = (bf16[96,1536]{1,0:T(8,128)(2,1)}, f32[16,128]{1,0:T(8,128)}) custom-call(bf16[384,896]{1,0:T(8,128)(2,1)} %bitcast.26, bf16[384,896]{1,0:T(8,128)(2,1)} %copy-done.4, bf16[3584,512]{1,0:T(8,128)(2,1)} %bitcast.31, bf16[3584,512]{1,0:T(8,128)(2,1)} %bitcast.33, bf16[512,3584]{1,0:T(8,128)(2,1)} %bitcast.35), custom_call_target="tpu_custom_call" | custom-call | tf_op jit(solution)/shard_map/home/pallas_call | solution.py:196
  77.6 6.9 %collective-permute-done.6.refs_2_ = bf16[384,896]{1,0:T(8,128)(2,1)} collective-permute-done((bf16[384,896]{1,0:T(8,128)(2,1)S(1)}, bf16[384,896]{1,0:T(8,128)(2,1)}, u32[]{:S(2)}, u32[]{:S(2)}) %collective-permute-start.6) | collective-permute-done | bytes 688160 | tf_op jit(solution)/shard_map/t_O/ppermute | solution.py:340
  84.5 1.5 %collective-permute-start.11 = (bf16[384,896]{1,0:T(8,128)(2,1)}, bf16[384,896]{1,0:T(8,128)(2,1)}, u32[]{:S(2)}, u32[]{:S(2)}) collective-permute-start(bf16[384,896]{1,0:T(8,128)(2,1)} %collective-permute-done.6.refs_2_), channel_id=1, source_target_pairs={{0,16},{16,0},{1,17},{17,1},{2,18},{18,2},{3,19},{19,3},{4,20},{20... | collective-permute-start | bytes 2064392 | tf_op jit(solution)/shard_map/t_xO/ppermute | solution.py:357
  86.0 0.1 collective-permute-start.9
  86.1 0.0 collective-permute-done.7.refs_3_
  86.1 0.0 collective-permute-done.8.refs_1_
  86.1 0.9 copy-done.6
  87.0 7.5 %home.3 = (bf16[96,1536]{1,0:T(8,128)(2,1)}, f32[16,128]{1,0:T(8,128)}) custom-call(bf16[384,896]{1,0:T(8,128)(2,1)} %bitcast.29, bf16[384,896]{1,0:T(8,128)(2,1)} %copy-done.6, bf16[3584,512]{1,0:T(8,128)(2,1)} %bitcast.32, bf16[3584,512]{1,0:T(8,128)(2,1)} %bitcast.34, bf16[512,3584]{1,0:T(8,128)(2,1)} %bitcast.36), custom_call_target="tpu_custom_call" | custom-call | tf_op jit(solution)/shard_map/home/pallas_call | solution.py:196
  94.5 3.0 %collective-permute-start.10 = (bf16[96,1536]{1,0:T(8,128)(2,1)}, bf16[96,1536]{1,0:T(8,128)(2,1)}, u32[]{:S(2)}, u32[]{:S(2)}) collective-permute-start(bf16[96,1536]{1,0:T(8,128)(2,1)} %get-tuple-element.46.refs_1_), channel_id=1, source_target_pairs={{0,8},{1,9},{2,10},{3,11},{4,12},{5,13},{6,14},{7,15},{8,0},{9,1},... | collective-permute-start | bytes 884744 | tf_op jit(solution)/shard_map/t_acts1/ppermute | solution.py:340
  97.5 0.7 broadcast_select_fusion.1
  98.2 0.6 pad_maximum_fusion.4
  98.8 4.4 %all-to-all-start.2 = ((f32[16,2,128]{2,1,0:T(2,128)}), f32[16,2,128]{2,1,0:T(2,128)S(1)}, u32[]{:S(2)}, u32[]{:S(2)}) async-start(f32[16,2,128]{2,1,0:T(2,128)} %pad_maximum_fusion.4), calls=%async_computation.2 | async-start | bytes 32768 | tf_op jit(solution)/shard_map/all_to_all | solution.py:389
  103.2 0.7 dynamic_slice.3.flag_ref
  103.9 0.0 collective-permute-done.11.refs_3_
  103.9 2.7 %sort_rows.2 = (bf16[4,96,896]{2,1,0:T(8,128)(2,1)S(1)}, bf16[4,96,896]{2,1,0:T(8,128)(2,1)S(1)}) custom-call(s32[1]{0:T(128)} %bitcast.place_ref.slot_ref, s32[1]{0:T(128)} %dynamic_slice.3.flag_ref, bf16[384,896]{1,0:T(8,128)(2,1)S(1)} %bitcast.27, bf16[384,896]{1,0:T(8,128)(2,1)S(1)} %copy-done.5, bf16[384,896]{1,0:T(8,128)(2,1)} %collective-permute-done.6.refs_2_, ...), custom_call_target="tpu_custom_call" | custom-call | tf_op jit(solution)/shard_map/sort_rows/pallas_call | solution.py:245
  106.6 0.0 copy-start.3
  106.6 1.1 copy-done.3
  107.7 1.1 copy-done.7
  108.8 2.9 %sort_rows.3 = (bf16[4,96,896]{2,1,0:T(8,128)(2,1)S(1)}, bf16[4,96,896]{2,1,0:T(8,128)(2,1)S(1)}) custom-call(s32[1]{0:T(128)} %bitcast.place_ref.slot_ref, s32[1]{0:T(128)} %dynamic_slice.3.flag_ref, bf16[384,896]{1,0:T(8,128)(2,1)S(1)} %bitcast.30, bf16[384,896]{1,0:T(8,128)(2,1)S(1)} %copy-done.7, ...), custom_call_target="tpu_custom_call" | custom-call | tf_op jit(solution)/shard_map/sort_rows/pallas_call | solution.py:245
  111.7 3.1 %all-to-all-done.2 = f32[16,2,128]{2,1,0:T(2,128)S(1)} async-done(((f32[16,2,128]{2,1,0:T(2,128)}), f32[16,2,128]{2,1,0:T(2,128)S(1)}, u32[]{:S(2)}, u32[]{:S(2)}) %all-to-all-start.2) | async-done | bytes 16416 | tf_op jit(solution)/shard_map/all_to_all | solution.py:389
  114.8 0.6 collective-permute-start.12
  115.5 0.0 collective-permute-done.10.refs_3_
  115.5 1.0 copy-done.8
  116.4 1.0 copy-done.9
  117.4 7.2 %grads.1 = (bf16[3584,512]{1,0:T(8,128)(2,1)}, bf16[3584,512]{1,0:T(8,128)(2,1)}, bf16[512,3584]{1,0:T(8,128)(2,1)}) custom-call(s32[1]{0:T(128)} %dynamic_slice.3.flag_ref, bf16[96,1536]{1,0:T(8,128)(2,1)S(1)} %copy-done.8, bf16[96,1536]{1,0:T(8,128)(2,1)S(1)} %copy-done.9, bf16[96,1536]{1,0:T(8,128)(2,1)} %collective-permute-done.9.refs_2_, ...), custom_call_target="tpu_custom_call" | custom-call | tf_op jit(solution)/shard_map/grads/pallas_call | solution.py:295
  124.6 0.1 broadcast_in_dim.28
  124.7 0.1 select_reduce_fusion
  124.8 0.6 bitcast_divide_fusion
  (38 shorter events, 0.3 us)
Async XLA Ops:
  6.0 24.8 %all-to-all-start = ((bf16[8,48,896]{2,1,0:T(8,128)(2,1)}), bf16[8,48,896]{2,1,0:T(8,128)(2,1)S(1)}, u32[]{:S(2)}, u32[]{:S(2)}) async-start(bf16[8,48,896]{2,1,0:T(8,128)(2,1)} %bitcast.37), calls=%async_computation | async-start | bytes 1376256 | tf_op jit(solution)/shard_map/t_A0/all_to_all | solution.py:333
  11.3 4.1 %collective-permute-start.2 = (bf16[192,896]{1,0:T(8,128)(2,1)}, bf16[192,896]{1,0:T(8,128)(2,1)S(1)}, u32[]{:S(2)}, u32[]{:S(2)}) collective-permute-start(bf16[192,896]{1,0:T(8,128)(2,1)} %get-tuple-element.38), channel_id=1, source_target_pairs={{0,1},{1,0},{2,3},{3,2},{4,5},{5,4},{6,7},{7,6},{8,9},{9,8},{10,11... | collective-permute-start | bytes 1032200 | tf_op jit(solution)/shard_map/t_A1c/ppermute | solution.py:340
  11.8 33.3 %collective-permute-start.1 = (bf16[384,896]{1,0:T(8,128)(2,1)}, bf16[384,896]{1,0:T(8,128)(2,1)}, u32[]{:S(2)}, u32[]{:S(2)}) collective-permute-start(bf16[384,896]{1,0:T(8,128)(2,1)} %get-tuple-element.36), channel_id=1, source_target_pairs={{0,8},{1,9},{2,10},{3,11},{4,12},{5,13},{6,14},{7,15},{8,0},{9,1},... | collective-permute-start | bytes 2064392 | tf_op jit(solution)/shard_map/t_M/ppermute | solution.py:340
  15.5 16.9 %collective-permute-start.3 = (bf16[96,896]{1,0:T(8,128)(2,1)S(1)}, bf16[96,896]{1,0:T(8,128)(2,1)S(1)}, u32[]{:S(2)}, u32[]{:S(2)}) collective-permute-start(bf16[96,896]{1,0:T(8,128)(2,1)S(1)} %pad_maximum_fusion.1), channel_id=1, source_target_pairs={{0,2},{1,3},{2,0},{3,1},{4,6},{5,7},{6,4},{7,5},{8,10},{9,11},{10,... | collective-permute-start | bytes 516104 | tf_op jit(solution)/shard_map/t_A11/ppermute | solution.py:340
  17.2 21.2 %collective-permute-start.4 = (bf16[96,896]{1,0:T(8,128)(2,1)S(1)}, bf16[96,896]{1,0:T(8,128)(2,1)S(1)}, u32[]{:S(2)}, u32[]{:S(2)}) collective-permute-start(bf16[96,896]{1,0:T(8,128)(2,1)S(1)} %pad_maximum_fusion.2), channel_id=1, source_target_pairs={{0,4},{1,5},{2,6},{3,7},{4,0},{5,1},{6,2},{7,3},{8,12},{9,13},{10,... | collective-permute-start | bytes 516104 | tf_op jit(solution)/shard_map/t_A12/ppermute | solution.py:340
  30.8 39.3 %copy-start = (bf16[8,48,896]{2,1,0:T(8,128)(2,1)}, bf16[8,48,896]{2,1,0:T(8,128)(2,1)S(1)}, u32[]{:S(2)}) copy-start(bf16[8,48,896]{2,1,0:T(8,128)(2,1)S(1)} %all-to-all-done) | copy-start | bytes 2064388
  30.8 16.6 %collective-permute-start = (bf16[384,896]{1,0:T(8,128)(2,1)S(1)}, bf16[384,896]{1,0:T(8,128)(2,1)S(1)}, u32[]{:S(2)}, u32[]{:S(2)}) collective-permute-start(bf16[384,896]{1,0:T(8,128)(2,1)S(1)} %bitcast.24), channel_id=1, source_target_pairs={{0,16},{16,0},{1,17},{17,1},{2,18},{18,2},{3,19},{19,3},{4,20},{20... | collective-permute-start | bytes 2064392 | tf_op jit(solution)/shard_map/t_xR0/ppermute | solution.py:357
  32.3 9.6 %collective-permute-start.5 = (bf16[96,896]{1,0:T(8,128)(2,1)S(1)}, bf16[96,896]{1,0:T(8,128)(2,1)S(1)}, u32[]{:S(2)}, u32[]{:S(2)}) collective-permute-start(bf16[96,896]{1,0:T(8,128)(2,1)S(1)} %pad_maximum_fusion.3), channel_id=1, source_target_pairs={{0,6},{1,7},{2,4},{3,5},{4,2},{5,3},{6,0},{7,1},{8,14},{9,15},{10,... | collective-permute-start | bytes 516104 | tf_op jit(solution)/shard_map/t_A13/ppermute | solution.py:340
  47.4 22.7 %copy-start.4 = (bf16[384,896]{1,0:T(8,128)(2,1)}, bf16[384,896]{1,0:T(8,128)(2,1)S(1)}, u32[]{:S(2)}) copy-start(bf16[384,896]{1,0:T(8,128)(2,1)S(1)} %collective-permute-done.refs_1_) | copy-start | bytes 2064388
  47.4 21.2 %all-to-all-start.1 = ((bf16[8,48,896]{2,1,0:T(8,128)(2,1)}), bf16[8,48,896]{2,1,0:T(8,128)(2,1)S(1)}, u32[]{:S(2)}, u32[]{:S(2)}) async-start(bf16[8,48,896]{2,1,0:T(8,128)(2,1)} %bitcast.8), calls=%async_computation.1 | async-start | bytes 1376256 | tf_op jit(solution)/shard_map/t_A2/all_to_all | solution.py:333
  51.0 33.5 %collective-permute-start.6 = (bf16[384,896]{1,0:T(8,128)(2,1)S(1)}, bf16[384,896]{1,0:T(8,128)(2,1)}, u32[]{:S(2)}, u32[]{:S(2)}) collective-permute-start(bf16[384,896]{1,0:T(8,128)(2,1)S(1)} %bitcast.25), channel_id=1, source_target_pairs={{0,8},{1,9},{2,10},{3,11},{4,12},{5,13},{6,14},{7,15},{8,0},{9,1},... | collective-permute-start | bytes 2064392 | tf_op jit(solution)/shard_map/t_O/ppermute | solution.py:340
  51.9 34.2 %collective-permute-start.7 = (bf16[384,896]{1,0:T(8,128)(2,1)S(1)}, bf16[384,896]{1,0:T(8,128)(2,1)}, u32[]{:S(2)}, u32[]{:S(2)}) collective-permute-start(bf16[384,896]{1,0:T(8,128)(2,1)S(1)} %constant_dynamic-update-slice_fusion.refs_2_), channel_id=1, source_target_pairs={{0,16},{16,0},{1,17},{17,1},{2,18},{18,2},{3,19},{19,3},{4,20},{20... | collective-permute-start | bytes 2064392 | tf_op jit(solution)/shard_map/t_xR1/ppermute | solution.py:357
  68.6 17.5 %copy-start.2 = (bf16[8,48,896]{2,1,0:T(8,128)(2,1)}, bf16[8,48,896]{2,1,0:T(8,128)(2,1)S(1)}, u32[]{:S(2)}) copy-start(bf16[8,48,896]{2,1,0:T(8,128)(2,1)S(1)} %all-to-all-done.1) | copy-start | bytes 2064388
  68.6 17.5 %collective-permute-start.8 = (bf16[384,896]{1,0:T(8,128)(2,1)S(1)}, bf16[384,896]{1,0:T(8,128)(2,1)S(1)}, u32[]{:S(2)}, u32[]{:S(2)}) collective-permute-start(bf16[384,896]{1,0:T(8,128)(2,1)S(1)} %bitcast.28), channel_id=1, source_target_pairs={{0,16},{16,0},{1,17},{17,1},{2,18},{18,2},{3,19},{19,3},{4,20},{20... | collective-permute-start | bytes 2064392 | tf_op jit(solution)/shard_map/t_xRM/ppermute | solution.py:357
  84.5 19.4 %collective-permute-start.11 = (bf16[384,896]{1,0:T(8,128)(2,1)}, bf16[384,896]{1,0:T(8,128)(2,1)}, u32[]{:S(2)}, u32[]{:S(2)}) collective-permute-start(bf16[384,896]{1,0:T(8,128)(2,1)} %collective-permute-done.6.refs_2_), channel_id=1, source_target_pairs={{0,16},{16,0},{1,17},{17,1},{2,18},{18,2},{3,19},{19,3},{4,20},{20... | collective-permute-start | bytes 2064392 | tf_op jit(solution)/shard_map/t_xO/ppermute | solution.py:357
  86.0 11.4 %copy-start.11 = (f32[16,128]{1,0:T(8,128)S(1)}, f32[16,128]{1,0:T(8,128)}, u32[]{:S(2)}) copy-start(f32[16,128]{1,0:T(8,128)} %get-tuple-element.57) | copy-start | bytes 24580
  86.0 17.2 %copy-start.13 = (s32[8]{0:T(128)S(1)}, s32[8]{0:T(128)}, u32[]{:S(2)}) copy-start(s32[8]{0:T(128)} %param.12) | copy-start | bytes 100
  86.0 17.9 %copy-start.1 = (bf16[8,48,896]{2,1,0:T(8,128)(2,1)S(1)}, bf16[8,48,896]{2,1,0:T(8,128)(2,1)}, u32[]{:S(2)}) copy-start(bf16[8,48,896]{2,1,0:T(8,128)(2,1)} %copy-done) | copy-start | bytes 2064388
  86.0 17.9 %copy-start.5 = (bf16[384,896]{1,0:T(8,128)(2,1)S(1)}, bf16[384,896]{1,0:T(8,128)(2,1)}, u32[]{:S(2)}) copy-start(bf16[384,896]{1,0:T(8,128)(2,1)} %copy-done.4) | copy-start | bytes 2064388
  86.0 29.4 %collective-permute-start.9 = (bf16[96,1536]{1,0:T(8,128)(2,1)}, bf16[96,1536]{1,0:T(8,128)(2,1)}, u32[]{:S(2)}, u32[]{:S(2)}) collective-permute-start(bf16[96,1536]{1,0:T(8,128)(2,1)} %get-tuple-element.47.refs_0_), channel_id=1, source_target_pairs={{0,8},{1,9},{2,10},{3,11},{4,12},{5,13},{6,14},{7,15},{8,0},{9,1},... | collective-permute-start | bytes 884744 | tf_op jit(solution)/shard_map/t_acts0/ppermute | solution.py:340
  86.1 0.9 copy-start.6
  94.5 21.0 %collective-permute-start.10 = (bf16[96,1536]{1,0:T(8,128)(2,1)}, bf16[96,1536]{1,0:T(8,128)(2,1)}, u32[]{:S(2)}, u32[]{:S(2)}) collective-permute-start(bf16[96,1536]{1,0:T(8,128)(2,1)} %get-tuple-element.46.refs_1_), channel_id=1, source_target_pairs={{0,8},{1,9},{2,10},{3,11},{4,12},{5,13},{6,14},{7,15},{8,0},{9,1},... | collective-permute-start | bytes 884744 | tf_op jit(solution)/shard_map/t_acts1/ppermute | solution.py:340
  98.8 16.1 %all-to-all-start.2 = ((f32[16,2,128]{2,1,0:T(2,128)}), f32[16,2,128]{2,1,0:T(2,128)S(1)}, u32[]{:S(2)}, u32[]{:S(2)}) async-start(f32[16,2,128]{2,1,0:T(2,128)} %pad_maximum_fusion.4), calls=%async_computation.2 | async-start | bytes 32768 | tf_op jit(solution)/shard_map/all_to_all | solution.py:389
  106.6 1.1 copy-start.3
  107.7 1.1 copy-start.7
  108.8 15.9 %copy-start.12 = (s32[8,128]{1,0:T(8,128)S(1)}, s32[8,128]{1,0:T(8,128)}, u32[]{:S(2)}) copy-start(s32[8,128]{1,0:T(8,128)} %get-tuple-element.56) | copy-start | bytes 12292
  108.8 16.0 %copy-start.10 = (bf16[128,8]{0,1:T(8,128)(2,1)S(1)}, bf16[128,8]{0,1:T(8,128)(2,1)}, u32[]{:S(2)}) copy-start(bf16[128,8]{0,1:T(8,128)(2,1)} %param.11) | copy-start | bytes 6148
  114.8 9.7 %collective-permute-start.12 = (f32[16,128]{1,0:T(8,128)S(1)}, f32[16,128]{1,0:T(8,128)S(1)}, u32[]{:S(2)}, u32[]{:S(2)}) collective-permute-start(f32[16,128]{1,0:T(8,128)S(1)} %bitcast.41), channel_id=1, source_target_pairs={{0,16},{16,0},{1,17},{17,1},{2,18},{18,2},{3,19},{19,3},{4,20},{20... | collective-permute-start | bytes 24584 | tf_op jit(solution)/shard_map/ppermute | solution.py:394
  115.5 1.0 copy-start.8
  116.4 1.0 copy-start.9

commit v2 on v1

--- a/solution.py
+++ b/solution.py
@@ -122,10 +122,17 @@
     return jnp.where(wanted == sub, 1.0, 0.0).astype(jnp.bfloat16)
 
 
-def home_kernel(half, wires, *refs):
+def home_kernel(half, wires, last, *refs):
+    if last:
+        slot_ref, plane_ref, flags_ref, near_ref, *refs = refs
+        slot_wires, refs = refs[:wires], refs[wires:]
     wire_refs = refs[:wires]
     sources = refs[wires : wires + 3]
-    acts_ref, score_ref, x_ref, s_ref, gate_ref, up_ref, down_ref, sems = refs[wires + 3 :]
+    acts_ref, score_ref, *refs = refs[wires + 3 :]
+    if last:
+        picked_x_ref, picked_s_ref, *refs = refs
+        picked_ref, *refs = refs
+    x_ref, s_ref, gate_ref, up_ref, down_ref, sems = refs
     rows = half * CAP
     quarter = wire_refs[0].shape[1]
     hidden_width = gate_ref.shape[1]
@@ -137,6 +144,12 @@
             copies.append(
                 pltpu.make_async_copy(source.at[place], target.at[place], sems.at[3 * q + n])
             )
+    if last:
+        low, side = slot_ref[0] % half, slot_ref[0] // half
+        taken = flags_ref[low] == 1
+        for w in range(wires):
+            fetch = pltpu.make_async_copy(slot_wires[w], picked_ref.at[w], sems.at[3 * CUTS + w])
+            pl.when(taken)(fetch.start)
     for copy in copies[: 3 * AHEAD]:
         copy.start()
     order = order_matrix(half, 0)
@@ -148,6 +161,28 @@
             place = (q, pl.ds(w * rows, rows))
             x_ref[place] = sorted_rows[q * rows : (q + 1) * rows]
             s_ref[place] = sorted_rows[(CUTS + q) * rows : (CUTS + q + 1) * rows]
+    if last:
+
+        @pl.when(taken)
+        def _():
+            turned = order_matrix(half, low)
+            for w in range(wires):
+                pltpu.make_async_copy(
+                    slot_wires[w], picked_ref.at[w], sems.at[3 * CUTS + w]
+                ).wait()
+                picked = jnp.dot(
+                    turned, picked_ref[w], preferred_element_type=jnp.float32
+                ).astype(jnp.bfloat16)
+                for q in range(CUTS):
+                    place = (q, pl.ds(w * rows, rows))
+                    picked_x_ref[place] = picked[q * rows : (q + 1) * rows]
+                    picked_s_ref[place] = picked[(CUTS + q) * rows : (CUTS + q + 1) * rows]
+
+        @pl.when(jnp.logical_not(taken))
+        def _():
+            picked_x_ref[...] = x_ref[...]
+            picked_s_ref[...] = s_ref[...]
+
     total = wires * rows
     pre_gate = pre_up = d_hidden = jnp.zeros((total, hidden_width), jnp.float32)
     for q in range(CUTS):
@@ -176,44 +211,60 @@
     lane = lax.broadcasted_iota(jnp.int32, (total, LANES), 1)
     spread = jnp.where(row == lane, score, 0.0)
     line = lax.broadcasted_iota(jnp.int32, (wires * half, 1), 0)
-    group = (line % wires) * rows + (line // wires) * CAP
+    group = (line // half) * rows + (line % half) * CAP
     member = lax.broadcasted_iota(jnp.int32, (wires * half, total), 1)
-    score_ref[...] = jnp.dot(
+    scores = jnp.dot(
         jnp.where((member >= group) & (member < group + CAP), 1.0, 0.0),
         spread,
         precision=lax.Precision.HIGHEST,
         preferred_element_type=jnp.float32,
     )
-
-
-def home(wires, w_gate, w_up, w_down, half):
-    width, hidden_width = w_gate.shape
+    if last:
+        for w in range(wires):
+            part = slice(w * half, (w + 1) * half)
+            first = 2 * half * ((plane_ref[0] - w + wires) % wires)
+            near_rows = pl.ds(pl.multiple_of(first + half * side, half), half)
+            far_rows = pl.ds(pl.multiple_of(first + half * (1 - side), half), half)
+            score_ref[near_rows, :] = near_ref[part, :]
+            score_ref[far_rows, :] = scores[part]
+    else:
+        score_ref[...] = scores
+
+
+def home(wires, weights, half, *more):
+    width, hidden_width = weights[0].shape
     count = len(wires)
     rows = count * half * CAP
     vmem = pl.BlockSpec(memory_space=pltpu.VMEM)
     hbm = pl.BlockSpec(memory_space=pltpu.HBM)
-    scratch = pltpu.VMEM((CUTS, rows, width // CUTS), jnp.bfloat16)
+    smem = pl.BlockSpec(memory_space=pltpu.SMEM)
+    parts = (CUTS, rows, width // CUTS)
+    scratch = pltpu.VMEM(parts, jnp.bfloat16)
+    out_shape = [
+        jax.ShapeDtypeStruct((rows, 3 * hidden_width), jnp.bfloat16),
+        jax.ShapeDtypeStruct((count * half * (2 if more else 1), LANES), jnp.float32),
+    ]
+    if more:
+        out_shape += [jax.ShapeDtypeStruct(parts, jnp.bfloat16)] * 2
     return pl.pallas_call(
-        functools.partial(home_kernel, half, count),
-        out_shape=(
-            jax.ShapeDtypeStruct((rows, 3 * hidden_width), jnp.bfloat16),
-            jax.ShapeDtypeStruct((count * half, LANES), jnp.float32),
-        ),
-        in_specs=[vmem] * count + [hbm] * 3,
-        out_specs=(vmem, vmem),
-        scratch_shapes=[scratch, scratch]
-        + [pltpu.VMEM(w.shape, jnp.bfloat16) for w in (w_gate, w_up, w_down)]
-        + [pltpu.SemaphoreType.DMA((3 * CUTS,))],
+        functools.partial(home_kernel, half, count, bool(more)),
+        out_shape=out_shape,
+        in_specs=([smem, smem, smem, vmem] + [hbm] * count if more else []) + [vmem] * count + [hbm] * 3,
+        out_specs=[vmem] * len(out_shape),
+        scratch_shapes=([pltpu.VMEM((count,) + wires[0].shape, jnp.bfloat16)] if more else [])
+        + [scratch, scratch]
+        + [pltpu.VMEM(w.shape, jnp.bfloat16) for w in weights]
+        + [pltpu.SemaphoreType.DMA((3 * CUTS + count,))],
         compiler_params=pltpu.CompilerParams(vmem_limit_bytes=56 * MIB),
-        name="home",
-    )(*wires, w_gate, w_up, w_down)
-
-
-def sort_kernel(half, wires, turns, slot_ref, flag_ref, *refs):
+        name="home_last" if more else "home",
+    )(*more, *wires, *weights)
+
+
+def sort_kernel(half, wires, slot_ref, flags_ref, *refs):
     own_wires, slot_wires = refs[:wires], refs[wires : 2 * wires]
     x_ref, s_ref, wire_ref, sems = refs[2 * wires :]
     rows = half * CAP
-    taken = flag_ref[0] == 1
+    taken = flags_ref[slot_ref[0] % half] == 1
 
     def fetch(w, source):
         pltpu.make_async_copy(source, wire_ref.at[w], sems.at[w]).start()
@@ -221,7 +272,7 @@
     for w in range(wires):
         pl.when(taken)(functools.partial(fetch, w, slot_wires[w]))
         pl.when(jnp.logical_not(taken))(functools.partial(fetch, w, own_wires[w]))
-    order = order_matrix(half, jnp.where(taken, slot_ref[0] % half, 0) if turns else 0)
+    order = order_matrix(half, 0)
     for w in range(wires):
         pltpu.make_async_copy(own_wires[w], wire_ref.at[w], sems.at[w]).wait()
         sorted_rows = jnp.dot(order, wire_ref[w], preferred_element_type=jnp.float32).astype(
@@ -234,7 +285,7 @@
             ]
 
 
-def sort_rows(slot, flag, own_wires, slot_wires, turns, half):
+def sort_rows(slot, flags, own_wires, slot_wires, half):
     count = len(own_wires)
     quarter = own_wires[0].shape[1]
     rows = count * half * CAP
@@ -243,7 +294,7 @@
     smem = pl.BlockSpec(memory_space=pltpu.SMEM)
     shape = jax.ShapeDtypeStruct((CUTS, rows, quarter), jnp.bfloat16)
     return pl.pallas_call(
-        functools.partial(sort_kernel, half, count, turns),
+        functools.partial(sort_kernel, half, count),
         out_shape=(shape, shape),
         in_specs=[smem, smem] + [hbm] * (2 * count),
         out_specs=(vmem, vmem),
@@ -251,25 +302,30 @@
             pltpu.VMEM((count, half * BLOCK, quarter), jnp.bfloat16),
             pltpu.SemaphoreType.DMA((count,)),
         ],
-        compiler_params=params(((rows, CUTS * quarter), 2 * 2), (own_wires[0].shape, 2 * count + 8)),
+        compiler_params=pltpu.CompilerParams(vmem_limit_bytes=56 * MIB),
         name="sort_rows",
-    )(slot, flag, *own_wires, *slot_wires)
-
-
-def grads_kernel(parts, flag_ref, *refs):
+    )(slot, flags, *own_wires, *slot_wires)
+
+
+def grads_kernel(half, parts, slot_ref, flags_ref, *refs):
     own_refs, other_refs = refs[:parts], refs[parts : 2 * parts]
     x_refs, s_refs = refs[2 * parts : 3 * parts], refs[3 * parts : 4 * parts]
-    gate_ref, up_ref, down_ref, acts_ref = refs[4 * parts :]
+    gate_ref, up_ref, down_ref, acts_ref, sems = refs[4 * parts :]
     rows = own_refs[0].shape[0]
     hidden_width = gate_ref.shape[1]
 
     @pl.when(pl.program_id(0) == 0)
     def _():
-        taken = flag_ref[0] == 1
+        taken = flags_ref[slot_ref[0] % half] == 1
         for p in range(parts):
-            acts_ref[pl.ds(p * rows, rows), :] = jnp.where(
-                taken, other_refs[p][...], own_refs[p][...]
+            target = acts_ref.at[pl.ds(p * rows, rows), :]
+            pl.when(taken)(pltpu.make_async_copy(other_refs[p], target, sems.at[p]).start)
+            pl.when(jnp.logical_not(taken))(
+                pltpu.make_async_copy(own_refs[p], target, sems.at[p]).start
             )
+        for p in range(parts):
+            target = acts_ref.at[pl.ds(p * rows, rows), :]
+            pltpu.make_async_copy(own_refs[p], target, sems.at[p]).wait()
 
     contract = (((0,), (0,)), ((), ()))
     x = jnp.concatenate([ref[0] for ref in x_refs], axis=0)
@@ -284,36 +340,36 @@
     ).astype(jnp.bfloat16)
 
 
-def grads(flag, own, other, x_parts, s_parts):
+def grads(slot, flags, own, other, x_parts, s_parts, half):
     count = len(own)
     cuts, rows, quarter = x_parts[0].shape
     width = cuts * quarter
     triple = own[0].shape[1]
     hidden_width = triple // 3
-    vmem = pl.BlockSpec(memory_space=pltpu.VMEM)
+    hbm = pl.BlockSpec(memory_space=pltpu.HBM)
+    smem = pl.BlockSpec(memory_space=pltpu.SMEM)
     part = pl.BlockSpec((1, rows, quarter), lambda q: (q, 0, 0))
     return pl.pallas_call(
-        functools.partial(grads_kernel, count),
+        functools.partial(grads_kernel, half, count),
         grid=(cuts,),
         out_shape=(
             jax.ShapeDtypeStruct((width, hidden_width), jnp.bfloat16),
             jax.ShapeDtypeStruct((width, hidden_width), jnp.bfloat16),
             jax.ShapeDtypeStruct((hidden_width, width), jnp.bfloat16),
         ),
-        in_specs=[pl.BlockSpec(memory_space=pltpu.SMEM)] + [vmem] * (2 * count) + [part] * (2 * count),
+        in_specs=[smem, smem] + [hbm] * (2 * count) + [part] * (2 * count),
         out_specs=(
             pl.BlockSpec((quarter, hidden_width), lambda q: (q, 0)),
             pl.BlockSpec((quarter, hidden_width), lambda q: (q, 0)),
             pl.BlockSpec((hidden_width, quarter), lambda q: (0, q)),
         ),
-        scratch_shapes=[pltpu.VMEM((count * rows, triple), jnp.bfloat16)],
-        compiler_params=params(
-            ((count * rows, triple), 3 * 2),
-            ((count * rows, quarter), 2 * 3 * 2),
-            ((quarter, hidden_width), 3 * (2 * 2 + 4)),
-        ),
+        scratch_shapes=[
+            pltpu.VMEM((count * rows, triple), jnp.bfloat16),
+            pltpu.SemaphoreType.DMA((count,)),
+        ],
+        compiler_params=pltpu.CompilerParams(vmem_limit_bytes=56 * MIB),
         name="grads",
-    )(flag, *own, *other, *x_parts, *s_parts)
+    )(slot, flags, *own, *other, *x_parts, *s_parts)
 
 
 def body(tokens, cotangent, expert_ids, gates, swap_flags, gate_w, up_w, down_w):
@@ -321,14 +377,13 @@
     planes = lax.axis_size("dp")
     half = axis_len // 2
     own_slot = lax.axis_index("expert")
-    side, low = own_slot // half, own_slot % half
     quarter = tokens.shape[1] // CUTS
     groups = [list(range(half)), list(range(half, axis_len))]
     slot = own_slot.reshape(1)
-    flag = lax.dynamic_slice_in_dim(swap_flags, low, 1, 0)
+    plane = lax.axis_index("dp").reshape(1)
 
     def exchange(wire, name):
-        with jax.named_scope("t_" + name):
+        with jax.named_scope(name):
             blocks = wire.reshape(half, BLOCK, quarter)
             moved = lax.all_to_all(
                 blocks, "expert", split_axis=0, concat_axis=0, tiled=True, axis_index_groups=groups
@@ -336,7 +391,7 @@
             return moved.reshape(half * BLOCK, quarter)
 
     def flip(block, by, name):
-        with jax.named_scope("t_" + name):
+        with jax.named_scope(name):
             return lax.ppermute(block, "expert", [(i, i ^ by) for i in range(axis_len)])
 
     def across(block, name):
@@ -352,7 +407,7 @@
         return jnp.concatenate(pieces, axis=0)
 
     def all_planes(wire, name):
-        with jax.named_scope("t_" + name):
+        with jax.named_scope(name):
             return [wire] + [
                 lax.ppermute(wire, "dp", [(i, (i + by) % planes) for i in range(planes)])
                 for by in range(1, planes)
@@ -364,40 +419,38 @@
     wire0, wire1, mine, theirs, pos = pack(
         slot, expert_ids.T, gates.T, tokens, cotangent, half
     )
-    moved = across(wire1, "M")
-    theirs = flip(theirs, 1, "A1c")
-    home0 = exchange(wire0, "A0")
-    homes0 = all_planes(home0, "xR0")
-    slot1 = turned_exchange(mine, theirs, "A1", ())
-    home1 = exchange(after(moved, slot1, *homes0[1:]), "A2")
-    crossed = across(after(home0, moved, *homes0[1:]), "O")
-    slots1 = all_planes(slot1, "xR1")
-    homes1 = all_planes(home1, "xRM")
+    moved = across(wire1, "rows_across")
+    theirs = flip(theirs, 1, "slot_rows_cores")
+    home0 = exchange(wire0, "home_rows_half")
+    homes0 = all_planes(home0, "home_rows_planes")
+    slot1 = turned_exchange(mine, theirs, "slot_rows_chips", ())
+    home1 = exchange(after(moved, slot1, *homes0[1:]), "crossed_rows_half")
+    crossed = across(after(home0, slot1), "home_rows_across")
+    slots1 = all_planes(slot1, "slot_rows_planes")
+    homes1 = all_planes(home1, "crossed_rows_planes")
     homes1[0] = after(homes1[0], crossed, *slots1[1:])
-    acts0, score0 = home(homes0, gate_w[0], up_w[0], down_w[0], half)
-    slots0 = all_planes(after(crossed, acts0), "xO")
-    acts1, score1 = home(homes1, gate_w[0], up_w[0], down_w[0], half)
+    weights = (gate_w[0], up_w[0], down_w[0])
+    acts0, score0 = home(homes0, weights, half)
+    slots0 = all_planes(after(crossed, acts0), "slot_crossed_planes")
+    acts1, back, x_rows1, s_rows1 = home(
+        homes1, weights, half, slot, plane, swap_flags, score0, *slots1
+    )
     own = [acts0, acts1]
-    other = [across(after(acts0, crossed), "acts0"), across(acts1, "acts1")]
-    rows0 = sort_rows(slot, flag, homes0, slots0, False, half)
-    rows1 = sort_rows(slot, flag, homes1, slots1, True, half)
-
-    near = score0.reshape(half, planes, LANES)
-    far = score1.reshape(half, planes, LANES)
-    near, far = lax.optimization_barrier((near, far) + ())[:2]
-    back = jnp.concatenate([jnp.where(side == 0, near, far), jnp.where(side == 0, far, near)])
-    returned = lax.all_to_all(back, "expert", split_axis=0, concat_axis=0, tiled=True)
-    returned = after(returned, rows0[0], rows1[0])
-    sums = [returned[:, 0]]
-    for by in range(1, planes):
-        sums.append(
-            lax.ppermute(returned[:, by], "dp", [(i, (i - by) % planes) for i in range(planes)])
-        )
-
+    other = [across(after(acts0, crossed), "acts_near_across"), across(acts1, "acts_far_across")]
+    x_rows0, s_rows0 = sort_rows(slot, swap_flags, homes0, slots0, half)
+
+    returned = lax.all_to_all(
+        back.reshape(planes * axis_len, 1, LANES),
+        ("dp", "expert"),
+        split_axis=0,
+        concat_axis=0,
+        tiled=True,
+    )
     out_gate, out_up, out_down = grads(
-        flag, own, other, [rows0[0], rows1[0]], [rows0[1], rows1[1]]
-    )
-    total = sum(lax.optimization_barrier((*sums, out_down))[:-1])
+        slot, swap_flags, own, other, [x_rows0, x_rows1], [s_rows0, s_rows1], half
+    )
+    returned = after(returned, out_down)
+    total = jnp.sum(returned.reshape(planes, axis_len, LANES), axis=0)
     values = total[:, :CAP].reshape(-1)
     match = pos[:, :, None] == jnp.arange(axis_len * CAP, dtype=jnp.int32)[None, None, :]
     picked = jnp.sum(jnp.where(match, values[None, None, :], 0.0), axis=2)

time: 126 us -> 124 us (0.984)
  waiting for transfers between devices: 52.1 us -> 57.5 us
  local copies, waits for them, and re-layouts: 6.91 us -> 2.84 us
  starting transfers between devices: 30.2 us -> 28 us
  other arithmetic: 2.1 us -> 0.79 us
    ppermute x8, waiting for transfers between devices: 19.5 us -> 26.9 us  [flip(): return lax.ppermute(block, 'expert', [(i, i ^ by) for i in range(axis_len)])]
    unnamed x31 -> x23, local copies, waits for them, and re-layouts: 5.06 us -> 1.66 us
    all_to_all x1, waiting for transfers between devices: 3.09 us -> 0.01 us  [body(): lax.all_to_all(back.reshape(planes * axis_len, 1, LANES), ('dp', 'expert'...]
    all_to_all x1, starting transfers between devices: 4.42 us -> 2.85 us  [body(): lax.all_to_all(back.reshape(planes * axis_len, 1, LANES), ('dp', 'expert'...]
    pallas_call x5 -> x4, Pallas kernels: 27.8 us -> 28.1 us  [the longest x2 15.9 us: home(): pl.pallas_call(functools.partial(home_kernel, half, count, bool(more)), o...]
  transfers between devices with their start and end apart: 16 -> 15, of which waited for: 8 -> 10; matrix products, arithmetic and copies ran while one was open for 3% -> 1% of each run, Pallas kernels for 22% -> 23%
where the time goes in v2:
time: 124 us
  waiting for transfers between devices  57.5 us (46%)
  Pallas kernels  33.5 us (27%)
  starting transfers between devices  28 us (23%)
  local copies, waits for them, and re-layouts  2.84 us (2%)
    all_to_all x2, waiting for transfers between devices, exchange(): lax.all_to_all(blocks, 'expert', split_axis=0, concat_axis=0, tiled=True,...  27.2 us
    ppermute x8, waiting for transfers between devices, flip(): return lax.ppermute(block, 'expert', [(i, i ^ by) for i in range(axis_len)])  26.9 us
    pallas_call x2, Pallas kernels, home(): pl.pallas_call(functools.partial(home_kernel, half, count, bool(more)), o...  15.9 us
    ppermute x8, starting transfers between devices, flip(): return lax.ppermute(block, 'expert', [(i, i ^ by) for i in range(axis_len)])  10.4 us
    all_to_all x2, starting transfers between devices, exchange(): lax.all_to_all(blocks, 'expert', split_axis=0, concat_axis=0, tiled=True,...  8.81 us
    pallas_call x1, Pallas kernels, grads(): pl.pallas_call(functools.partial(grads_kernel, half, count), grid=(cuts,)...  8.26 us
    ppermute x4, starting transfers between devices, all_planes(): lax.ppermute(wire, 'dp', [(i, (i + by) % planes) for i in range(planes)])  5.99 us
    pallas_call x1, Pallas kernels, pack(): pl.pallas_call(functools.partial(pack_kernel, half), out_shape=(wire, wir...  5.36 us
  transfers between devices with their start and end apart: 15, of which 10 were waited for; matrix products, arithmetic and copies ran while one was open for 1% of the time, Pallas kernels for 23%

profile of v2, /device:TPU:0, one launch (start us, length us, event | category | flops | bytes accessed | tf_op | source)
XLA Modules:
  0.0 123.5 jit_solution(15402586604210909419)
XLA Ops:
  0.6 5.4 %pack.1 = (bf16[384,896]{1,0:T(8,128)(2,1)}, bf16[384,896]{1,0:T(8,128)(2,1)}, bf16[192,896]{1,0:T(8,128)(2,1)}, bf16[192,896]{1,0:T(8,128)(2,1)}, s32[8,128]{1,0:T(8,128)}) custom-call(s32[1]{0:T(128)} %bitcast.place_ref.refs_0_.slot_ref, s32[8,128]{1,0:T(8,128)} %bitcast.40, bf16[8,128]{1,0:T(8,128)(2,1)} %bitcast.39, bf16[128,3584]{1,0:T(8,128)(2,1)} %tokens_ref.1, ...), custom_call_target="tpu_custom_call" | custom-call | tf_op jit(solution)/shard_map/pack/pallas_call | solution.py:102
  6.0 5.3 %all-to-all-start = ((bf16[8,48,896]{2,1,0:T(8,128)(2,1)}), bf16[8,48,896]{2,1,0:T(8,128)(2,1)S(1)}, u32[]{:S(2)}, u32[]{:S(2)}) async-start(bf16[8,48,896]{2,1,0:T(8,128)(2,1)} %bitcast.35), calls=%async_computation | async-start | bytes 1376256 | tf_op jit(solution)/shard_map/home_rows_half/all_to_all | solution.py:388
  11.3 0.5 collective-permute-start.1
  11.8 2.6 %collective-permute-start.6 = (bf16[384,896]{1,0:T(8,128)(2,1)}, bf16[384,896]{1,0:T(8,128)(2,1)}, u32[]{:S(2)}, u32[]{:S(2)}) collective-permute-start(bf16[384,896]{1,0:T(8,128)(2,1)} %get-tuple-element.39), channel_id=1, source_target_pairs={{0,8},{1,9},{2,10},{3,11},{4,12},{5,13},{6,14},{7,15},{8,0},{9,1},... | collective-permute-start | bytes 2064392 | tf_op jit(solution)/shard_map/rows_across/ppermute | solution.py:395
  14.4 1.0 fusion
  15.4 0.0 collective-permute-done.1
  15.5 1.7 %collective-permute-start.2 = (bf16[96,896]{1,0:T(8,128)(2,1)S(1)}, bf16[96,896]{1,0:T(8,128)(2,1)S(1)}, u32[]{:S(2)}, u32[]{:S(2)}) collective-permute-start(bf16[96,896]{1,0:T(8,128)(2,1)S(1)} %pad_maximum_fusion.1), channel_id=1, source_target_pairs={{0,2},{1,3},{2,0},{3,1},{4,6},{5,7},{6,4},{7,5},{8,10},{9,11},{10,... | collective-permute-start | bytes 516104 | tf_op jit(solution)/shard_map/slot_rows_chips1/ppermute | solution.py:395
  17.2 1.5 %collective-permute-start.3 = (bf16[96,896]{1,0:T(8,128)(2,1)S(1)}, bf16[96,896]{1,0:T(8,128)(2,1)S(1)}, u32[]{:S(2)}, u32[]{:S(2)}) collective-permute-start(bf16[96,896]{1,0:T(8,128)(2,1)S(1)} %pad_maximum_fusion.2), channel_id=1, source_target_pairs={{0,4},{1,5},{2,6},{3,7},{4,0},{5,1},{6,2},{7,3},{8,12},{9,13},{10,... | collective-permute-start | bytes 516104 | tf_op jit(solution)/shard_map/slot_rows_chips2/ppermute | solution.py:395
  18.8 12.0 %all-to-all-done = bf16[8,48,896]{2,1,0:T(8,128)(2,1)S(1)} async-done(((bf16[8,48,896]{2,1,0:T(8,128)(2,1)}), bf16[8,48,896]{2,1,0:T(8,128)(2,1)S(1)}, u32[]{:S(2)}, u32[]{:S(2)}) %all-to-all-start) | async-done | bytes 688160 | tf_op jit(solution)/shard_map/home_rows_half/all_to_all | solution.py:388
  30.8 1.5 %collective-permute-start = (bf16[384,896]{1,0:T(8,128)(2,1)S(1)}, bf16[384,896]{1,0:T(8,128)(2,1)S(1)}, u32[]{:S(2)}, u32[]{:S(2)}) collective-permute-start(bf16[384,896]{1,0:T(8,128)(2,1)S(1)} %bitcast.29), channel_id=1, source_target_pairs={{0,16},{16,0},{1,17},{17,1},{2,18},{18,2},{3,19},{19,3},{4,20},{20... | collective-permute-start | bytes 2064392 | tf_op jit(solution)/shard_map/home_rows_planes/ppermute | solution.py:412
  32.3 0.1 collective-permute-start.4
  32.4 0.0 collective-permute-done.2
  32.4 6.0 %collective-permute-done.3 = bf16[96,896]{1,0:T(8,128)(2,1)S(1)} collective-permute-done((bf16[96,896]{1,0:T(8,128)(2,1)S(1)}, bf16[96,896]{1,0:T(8,128)(2,1)S(1)}, u32[]{:S(2)}, u32[]{:S(2)}) %collective-permute-start.3) | collective-permute-done | bytes 172064 | tf_op jit(solution)/shard_map/slot_rows_chips2/ppermute | solution.py:395
  38.5 3.5 %collective-permute-done.4 = bf16[96,896]{1,0:T(8,128)(2,1)S(1)} collective-permute-done((bf16[96,896]{1,0:T(8,128)(2,1)S(1)}, bf16[96,896]{1,0:T(8,128)(2,1)S(1)}, u32[]{:S(2)}, u32[]{:S(2)}) %collective-permute-start.4) | collective-permute-done | bytes 172064 | tf_op jit(solution)/shard_map/slot_rows_chips3/ppermute | solution.py:395
  42.1 0.0 copy-start.3
  42.1 3.0 %collective-permute-done.6 = bf16[384,896]{1,0:T(8,128)(2,1)} collective-permute-done((bf16[384,896]{1,0:T(8,128)(2,1)}, bf16[384,896]{1,0:T(8,128)(2,1)}, u32[]{:S(2)}, u32[]{:S(2)}) %collective-permute-start.6) | collective-permute-done | bytes 688160 | tf_op jit(solution)/shard_map/rows_across/ppermute | solution.py:395
  45.1 2.3 %collective-permute-done.refs_1_ = bf16[384,896]{1,0:T(8,128)(2,1)S(1)} collective-permute-done((bf16[384,896]{1,0:T(8,128)(2,1)S(1)}, bf16[384,896]{1,0:T(8,128)(2,1)S(1)}, u32[]{:S(2)}, u32[]{:S(2)}) %collective-permute-start) | collective-permute-done | bytes 688160 | tf_op jit(solution)/shard_map/home_rows_planes/ppermute | solution.py:412
  47.4 3.5 %all-to-all-start.1 = ((bf16[8,48,896]{2,1,0:T(8,128)(2,1)}), bf16[8,48,896]{2,1,0:T(8,128)(2,1)S(1)}, u32[]{:S(2)}, u32[]{:S(2)}) async-start(bf16[8,48,896]{2,1,0:T(8,128)(2,1)} %bitcast.9), calls=%async_computation.1 | async-start | bytes 1376256 | tf_op jit(solution)/shard_map/crossed_rows_half/all_to_all | solution.py:388
  51.0 0.9 collective-permute-start.7
  51.9 1.5 %collective-permute-start.5 = (bf16[384,896]{1,0:T(8,128)(2,1)S(1)}, bf16[384,896]{1,0:T(8,128)(2,1)}, u32[]{:S(2)}, u32[]{:S(2)}) collective-permute-start(bf16[384,896]{1,0:T(8,128)(2,1)S(1)} %constant_dynamic-update-slice_fusion.refs_4_), channel_id=1, source_target_pairs={{0,16},{16,0},{1,17},{17,1},{2,18},{18,2},{3,19},{19,3},{4,20},{20... | collective-permute-start | bytes 2064392 | tf_op jit(solution)/shard_map/slot_rows_planes/ppermute | solution.py:412
  53.4 15.2 %all-to-all-done.1 = bf16[8,48,896]{2,1,0:T(8,128)(2,1)S(1)} async-done(((bf16[8,48,896]{2,1,0:T(8,128)(2,1)}), bf16[8,48,896]{2,1,0:T(8,128)(2,1)S(1)}, u32[]{:S(2)}, u32[]{:S(2)}) %all-to-all-start.1) | async-done | bytes 688160 | tf_op jit(solution)/shard_map/crossed_rows_half/all_to_all | solution.py:388
  68.6 1.5 %collective-permute-start.8 = (bf16[384,896]{1,0:T(8,128)(2,1)S(1)}, bf16[384,896]{1,0:T(8,128)(2,1)}, u32[]{:S(2)}, u32[]{:S(2)}) collective-permute-start(bf16[384,896]{1,0:T(8,128)(2,1)S(1)} %bitcast.33), channel_id=1, source_target_pairs={{0,16},{16,0},{1,17},{17,1},{2,18},{18,2},{3,19},{19,3},{4,20},{20... | collective-permute-start | bytes 2064392 | tf_op jit(solution)/shard_map/crossed_rows_planes/ppermute | solution.py:412
  70.1 0.0 copy-done
  70.1 0.0 copy-done.1
  70.1 7.5 %home.1 = (bf16[96,1536]{1,0:T(8,128)(2,1)}, f32[16,128]{1,0:T(8,128)}) custom-call(bf16[384,896]{1,0:T(8,128)(2,1)} %bitcast.31, bf16[384,896]{1,0:T(8,128)(2,1)} %copy-done.1, bf16[3584,512]{1,0:T(8,128)(2,1)} %bitcast.23, bf16[3584,512]{1,0:T(8,128)(2,1)} %bitcast.25, bf16[512,3584]{1,0:T(8,128)(2,1)} %bitcast.27), custom_call_target="tpu_custom_call" | custom-call | tf_op jit(solution)/shard_map/home/pallas_call | solution.py:249
  77.7 0.0 copy-done.3
  77.7 0.0 copy-done.2
  77.7 6.7 %collective-permute-done.7.refs_2_ = bf16[384,896]{1,0:T(8,128)(2,1)S(1)} collective-permute-done((bf16[384,896]{1,0:T(8,128)(2,1)S(1)}, bf16[384,896]{1,0:T(8,128)(2,1)S(1)}, u32[]{:S(2)}, u32[]{:S(2)}) %collective-permute-start.7) | collective-permute-done | bytes 688160 | tf_op jit(solution)/shard_map/home_rows_across/ppermute | solution.py:395
  84.4 1.5 %collective-permute-start.11 = (bf16[384,896]{1,0:T(8,128)(2,1)S(1)}, bf16[384,896]{1,0:T(8,128)(2,1)S(1)}, u32[]{:S(2)}, u32[]{:S(2)}) collective-permute-start(bf16[384,896]{1,0:T(8,128)(2,1)S(1)} %collective-permute-done.7.refs_2_), channel_id=1, source_target_pairs={{0,16},{16,0},{1,17},{17,1},{2,18},{18,2},{3,19},{19,3},{4,20},{20... | collective-permute-start | bytes 2064392 | tf_op jit(solution)/shard_map/slot_crossed_planes/ppermute | solution.py:412
  85.9 0.0 collective-permute-start.9
  85.9 0.0 collective-permute-done.5.refs_5_
  85.9 0.0 collective-permute-done.8.refs_7_
  85.9 8.4 %home_last.1 = (bf16[96,1536]{1,0:T(8,128)(2,1)}, f32[32,128]{1,0:T(8,128)}, bf16[4,96,896]{2,1,0:T(8,128)(2,1)}, bf16[4,96,896]{2,1,0:T(8,128)(2,1)}) custom-call(s32[1]{0:T(128)} %bitcast.place_ref.refs_0_.slot_ref, s32[1]{0:T(128)} %bitcast.8.refs_1_, s32[8]{0:T(128)} %flags_ref.3, f32[16,128]{1,0:T(8,128)} %get-tuple-element.32.refs_3_, ...), custom_call_target="tpu_custom_call" | custom-call | tf_op jit(solution)/shard_map/home_last/pallas_call | solution.py:249
  94.3 0.0 copy-start.9
  94.3 0.0 copy-start.8
  94.4 3.0 %collective-permute-start.10 = (bf16[96,1536]{1,0:T(8,128)(2,1)}, bf16[96,1536]{1,0:T(8,128)(2,1)S(1)}, u32[]{:S(2)}, u32[]{:S(2)}) collective-permute-start(bf16[96,1536]{1,0:T(8,128)(2,1)} %get-tuple-element.43.refs_1_), channel_id=1, source_target_pairs={{0,8},{1,9},{2,10},{3,11},{4,12},{5,13},{6,14},{7,15},{8,0},{9,1},... | collective-permute-start | bytes 884744 | tf_op jit(solution)/shard_map/acts_far_across/ppermute | solution.py:395
  97.3 2.9 %all-to-all-start.2 = ((f32[32,1,128]{2,1,0:T(1,128)}), f32[32,1,128]{2,1,0:T(1,128)S(1)}, u32[]{:S(2)}, u32[]{:S(2)}) async-start(f32[32,1,128]{2,1,0:T(1,128)} %bitcast.38), calls=%async_computation.2 | async-start | bytes 32768 | tf_op jit(solution)/shard_map/all_to_all | solution.py:442
  100.2 1.1 collective-permute-done.11.refs_3_
  101.3 0.8 copy-done.5
  102.1 4.0 %sort_rows.1 = (bf16[4,96,896]{2,1,0:T(8,128)(2,1)}, bf16[4,96,896]{2,1,0:T(8,128)(2,1)}) custom-call(s32[1]{0:T(128)} %bitcast.place_ref.refs_0_.slot_ref, s32[8]{0:T(128)} %flags_ref.3, bf16[384,896]{1,0:T(8,128)(2,1)} %bitcast.32, bf16[384,896]{1,0:T(8,128)(2,1)} %copy-done.1, bf16[384,896]{1,0:T(8,128)(2,1)} %copy-done.4, bf16[384,896]{1,0:T(8,128)(2,1)} %copy-done.5), custom_call_target="tpu_custom_call" | custom-call | tf_op jit(solution)/shard_map/sort_rows/pallas_call | solution.py:296
  106.1 1.3 %collective-permute-done.9.refs_2_ = bf16[96,1536]{1,0:T(8,128)(2,1)S(1)} collective-permute-done((bf16[96,1536]{1,0:T(8,128)(2,1)}, bf16[96,1536]{1,0:T(8,128)(2,1)S(1)}, u32[]{:S(2)}, u32[]{:S(2)}) %collective-permute-start.9) | collective-permute-done | bytes 294944 | tf_op jit(solution)/shard_map/acts_near_across/ppermute | solution.py:395
  107.4 6.3 %collective-permute-done.10.refs_3_ = bf16[96,1536]{1,0:T(8,128)(2,1)S(1)} collective-permute-done((bf16[96,1536]{1,0:T(8,128)(2,1)}, bf16[96,1536]{1,0:T(8,128)(2,1)S(1)}, u32[]{:S(2)}, u32[]{:S(2)}) %collective-permute-start.10) | collective-permute-done | bytes 294944 | tf_op jit(solution)/shard_map/acts_far_across/ppermute | solution.py:395
  113.7 0.7 copy-done.7
  114.4 8.3 %grads.1 = (bf16[3584,512]{1,0:T(8,128)(2,1)}, bf16[3584,512]{1,0:T(8,128)(2,1)}, bf16[512,3584]{1,0:T(8,128)(2,1)}) custom-call(s32[1]{0:T(128)} %bitcast.place_ref.refs_0_.slot_ref, s32[8]{0:T(128)} %flags_ref.3, bf16[96,1536]{1,0:T(8,128)(2,1)} %get-tuple-element.44.refs_0_, bf16[96,1536]{1,0:T(8,128)(2,1)} %get-tuple-element.43.refs_1_, ...), custom_call_target="tpu_custom_call" | custom-call | tf_op jit(solution)/shard_map/grads/pallas_call | solution.py:352
  122.7 0.0 all-to-all-done.2
  122.7 0.1 broadcast_in_dim.28
  122.8 0.1 select_reduce_fusion
  122.9 0.6 bitcast_divide_fusion
  (21 shorter events, 0.2 us)
Async XLA Ops:
  6.0 24.8 %all-to-all-start = ((bf16[8,48,896]{2,1,0:T(8,128)(2,1)}), bf16[8,48,896]{2,1,0:T(8,128)(2,1)S(1)}, u32[]{:S(2)}, u32[]{:S(2)}) async-start(bf16[8,48,896]{2,1,0:T(8,128)(2,1)} %bitcast.35), calls=%async_computation | async-start | bytes 1376256 | tf_op jit(solution)/shard_map/home_rows_half/all_to_all | solution.py:388
  11.3 4.1 %collective-permute-start.1 = (bf16[192,896]{1,0:T(8,128)(2,1)}, bf16[192,896]{1,0:T(8,128)(2,1)S(1)}, u32[]{:S(2)}, u32[]{:S(2)}) collective-permute-start(bf16[192,896]{1,0:T(8,128)(2,1)} %get-tuple-element.34), channel_id=1, source_target_pairs={{0,1},{1,0},{2,3},{3,2},{4,5},{5,4},{6,7},{7,6},{8,9},{9,8},{10,11... | collective-permute-start | bytes 1032200 | tf_op jit(solution)/shard_map/slot_rows_cores/ppermute | solution.py:395
  11.8 33.3 %collective-permute-start.6 = (bf16[384,896]{1,0:T(8,128)(2,1)}, bf16[384,896]{1,0:T(8,128)(2,1)}, u32[]{:S(2)}, u32[]{:S(2)}) collective-permute-start(bf16[384,896]{1,0:T(8,128)(2,1)} %get-tuple-element.39), channel_id=1, source_target_pairs={{0,8},{1,9},{2,10},{3,11},{4,12},{5,13},{6,14},{7,15},{8,0},{9,1},... | collective-permute-start | bytes 2064392 | tf_op jit(solution)/shard_map/rows_across/ppermute | solution.py:395
  15.5 17.0 %collective-permute-start.2 = (bf16[96,896]{1,0:T(8,128)(2,1)S(1)}, bf16[96,896]{1,0:T(8,128)(2,1)S(1)}, u32[]{:S(2)}, u32[]{:S(2)}) collective-permute-start(bf16[96,896]{1,0:T(8,128)(2,1)S(1)} %pad_maximum_fusion.1), channel_id=1, source_target_pairs={{0,2},{1,3},{2,0},{3,1},{4,6},{5,7},{6,4},{7,5},{8,10},{9,11},{10,... | collective-permute-start | bytes 516104 | tf_op jit(solution)/shard_map/slot_rows_chips1/ppermute | solution.py:395
  17.2 21.2 %collective-permute-start.3 = (bf16[96,896]{1,0:T(8,128)(2,1)S(1)}, bf16[96,896]{1,0:T(8,128)(2,1)S(1)}, u32[]{:S(2)}, u32[]{:S(2)}) collective-permute-start(bf16[96,896]{1,0:T(8,128)(2,1)S(1)} %pad_maximum_fusion.2), channel_id=1, source_target_pairs={{0,4},{1,5},{2,6},{3,7},{4,0},{5,1},{6,2},{7,3},{8,12},{9,13},{10,... | collective-permute-start | bytes 516104 | tf_op jit(solution)/shard_map/slot_rows_chips2/ppermute | solution.py:395
  30.8 39.3 %copy-start = (bf16[8,48,896]{2,1,0:T(8,128)(2,1)}, bf16[8,48,896]{2,1,0:T(8,128)(2,1)S(1)}, u32[]{:S(2)}) copy-start(bf16[8,48,896]{2,1,0:T(8,128)(2,1)S(1)} %all-to-all-done) | copy-start | bytes 2064388
  30.8 16.6 %collective-permute-start = (bf16[384,896]{1,0:T(8,128)(2,1)S(1)}, bf16[384,896]{1,0:T(8,128)(2,1)S(1)}, u32[]{:S(2)}, u32[]{:S(2)}) collective-permute-start(bf16[384,896]{1,0:T(8,128)(2,1)S(1)} %bitcast.29), channel_id=1, source_target_pairs={{0,16},{16,0},{1,17},{17,1},{2,18},{18,2},{3,19},{19,3},{4,20},{20... | collective-permute-start | bytes 2064392 | tf_op jit(solution)/shard_map/home_rows_planes/ppermute | solution.py:412
  32.3 9.6 %collective-permute-start.4 = (bf16[96,896]{1,0:T(8,128)(2,1)S(1)}, bf16[96,896]{1,0:T(8,128)(2,1)S(1)}, u32[]{:S(2)}, u32[]{:S(2)}) collective-permute-start(bf16[96,896]{1,0:T(8,128)(2,1)S(1)} %pad_maximum_fusion.3), channel_id=1, source_target_pairs={{0,6},{1,7},{2,4},{3,5},{4,2},{5,3},{6,0},{7,1},{8,14},{9,15},{10,... | collective-permute-start | bytes 516104 | tf_op jit(solution)/shard_map/slot_rows_chips3/ppermute | solution.py:395
  42.1 35.6 %copy-start.3 = (bf16[384,896]{1,0:T(8,128)(2,1)}, bf16[384,896]{1,0:T(8,128)(2,1)S(1)}, u32[]{:S(2)}) copy-start(bf16[384,896]{1,0:T(8,128)(2,1)S(1)} %constant_dynamic-update-slice_fusion.refs_4_) | copy-start | bytes 2064388
  47.4 22.7 %copy-start.1 = (bf16[384,896]{1,0:T(8,128)(2,1)}, bf16[384,896]{1,0:T(8,128)(2,1)S(1)}, u32[]{:S(2)}) copy-start(bf16[384,896]{1,0:T(8,128)(2,1)S(1)} %collective-permute-done.refs_1_) | copy-start | bytes 2064388
  47.4 21.2 %all-to-all-start.1 = ((bf16[8,48,896]{2,1,0:T(8,128)(2,1)}), bf16[8,48,896]{2,1,0:T(8,128)(2,1)S(1)}, u32[]{:S(2)}, u32[]{:S(2)}) async-start(bf16[8,48,896]{2,1,0:T(8,128)(2,1)} %bitcast.9), calls=%async_computation.1 | async-start | bytes 1376256 | tf_op jit(solution)/shard_map/crossed_rows_half/all_to_all | solution.py:388
  51.0 33.4 %collective-permute-start.7 = (bf16[384,896]{1,0:T(8,128)(2,1)S(1)}, bf16[384,896]{1,0:T(8,128)(2,1)S(1)}, u32[]{:S(2)}, u32[]{:S(2)}) collective-permute-start(bf16[384,896]{1,0:T(8,128)(2,1)S(1)} %bitcast.30), channel_id=1, source_target_pairs={{0,8},{1,9},{2,10},{3,11},{4,12},{5,13},{6,14},{7,15},{8,0},{9,1},... | collective-permute-start | bytes 2064392 | tf_op jit(solution)/shard_map/home_rows_across/ppermute | solution.py:395
  51.9 34.0 %collective-permute-start.5 = (bf16[384,896]{1,0:T(8,128)(2,1)S(1)}, bf16[384,896]{1,0:T(8,128)(2,1)}, u32[]{:S(2)}, u32[]{:S(2)}) collective-permute-start(bf16[384,896]{1,0:T(8,128)(2,1)S(1)} %constant_dynamic-update-slice_fusion.refs_4_), channel_id=1, source_target_pairs={{0,16},{16,0},{1,17},{17,1},{2,18},{18,2},{3,19},{19,3},{4,20},{20... | collective-permute-start | bytes 2064392 | tf_op jit(solution)/shard_map/slot_rows_planes/ppermute | solution.py:412
  68.6 9.0 %copy-start.2 = (bf16[8,48,896]{2,1,0:T(8,128)(2,1)}, bf16[8,48,896]{2,1,0:T(8,128)(2,1)S(1)}, u32[]{:S(2)}) copy-start(bf16[8,48,896]{2,1,0:T(8,128)(2,1)S(1)} %all-to-all-done.1) | copy-start | bytes 2064388
  68.6 17.3 %collective-permute-start.8 = (bf16[384,896]{1,0:T(8,128)(2,1)S(1)}, bf16[384,896]{1,0:T(8,128)(2,1)}, u32[]{:S(2)}, u32[]{:S(2)}) collective-permute-start(bf16[384,896]{1,0:T(8,128)(2,1)S(1)} %bitcast.33), channel_id=1, source_target_pairs={{0,16},{16,0},{1,17},{17,1},{2,18},{18,2},{3,19},{19,3},{4,20},{20... | collective-permute-start | bytes 2064392 | tf_op jit(solution)/shard_map/crossed_rows_planes/ppermute | solution.py:412
  84.4 9.9 %copy-start.4 = (bf16[384,896]{1,0:T(8,128)(2,1)}, bf16[384,896]{1,0:T(8,128)(2,1)S(1)}, u32[]{:S(2)}) copy-start(bf16[384,896]{1,0:T(8,128)(2,1)S(1)} %collective-permute-done.7.refs_2_) | copy-start | bytes 2064388
  84.4 16.9 %collective-permute-start.11 = (bf16[384,896]{1,0:T(8,128)(2,1)S(1)}, bf16[384,896]{1,0:T(8,128)(2,1)S(1)}, u32[]{:S(2)}, u32[]{:S(2)}) collective-permute-start(bf16[384,896]{1,0:T(8,128)(2,1)S(1)} %collective-permute-done.7.refs_2_), channel_id=1, source_target_pairs={{0,16},{16,0},{1,17},{17,1},{2,18},{18,2},{3,19},{19,3},{4,20},{20... | collective-permute-start | bytes 2064392 | tf_op jit(solution)/shard_map/slot_crossed_planes/ppermute | solution.py:412
  85.9 21.5 %collective-permute-start.9 = (bf16[96,1536]{1,0:T(8,128)(2,1)}, bf16[96,1536]{1,0:T(8,128)(2,1)S(1)}, u32[]{:S(2)}, u32[]{:S(2)}) collective-permute-start(bf16[96,1536]{1,0:T(8,128)(2,1)} %get-tuple-element.44.refs_0_), channel_id=1, source_target_pairs={{0,8},{1,9},{2,10},{3,11},{4,12},{5,13},{6,14},{7,15},{8,0},{9,1},... | collective-permute-start | bytes 884744 | tf_op jit(solution)/shard_map/acts_near_across/ppermute | solution.py:395
  94.3 28.5 %copy-start.9 = (s32[8,128]{1,0:T(8,128)S(1)}, s32[8,128]{1,0:T(8,128)}, u32[]{:S(2)}) copy-start(s32[8,128]{1,0:T(8,128)} %get-tuple-element.53) | copy-start | bytes 12292
  94.3 28.6 %copy-start.8 = (bf16[128,8]{0,1:T(8,128)(2,1)S(1)}, bf16[128,8]{0,1:T(8,128)(2,1)}, u32[]{:S(2)}) copy-start(bf16[128,8]{0,1:T(8,128)(2,1)} %param.11) | copy-start | bytes 6148
  94.4 19.3 %collective-permute-start.10 = (bf16[96,1536]{1,0:T(8,128)(2,1)}, bf16[96,1536]{1,0:T(8,128)(2,1)S(1)}, u32[]{:S(2)}, u32[]{:S(2)}) collective-permute-start(bf16[96,1536]{1,0:T(8,128)(2,1)} %get-tuple-element.43.refs_1_), channel_id=1, source_target_pairs={{0,8},{1,9},{2,10},{3,11},{4,12},{5,13},{6,14},{7,15},{8,0},{9,1},... | collective-permute-start | bytes 884744 | tf_op jit(solution)/shard_map/acts_far_across/ppermute | solution.py:395
  97.3 25.3 %all-to-all-start.2 = ((f32[32,1,128]{2,1,0:T(1,128)}), f32[32,1,128]{2,1,0:T(1,128)S(1)}, u32[]{:S(2)}, u32[]{:S(2)}) async-start(f32[32,1,128]{2,1,0:T(1,128)} %bitcast.38), calls=%async_computation.2 | async-start | bytes 32768 | tf_op jit(solution)/shard_map/all_to_all | solution.py:442
  101.3 0.8 copy-start.5
  107.4 6.3 %copy-start.6 = (bf16[96,1536]{1,0:T(8,128)(2,1)}, bf16[96,1536]{1,0:T(8,128)(2,1)S(1)}, u32[]{:S(2)}) copy-start(bf16[96,1536]{1,0:T(8,128)(2,1)S(1)} %collective-permute-done.9.refs_2_) | copy-start | bytes 884740
  113.7 0.7 copy-start.7

commit v3 on v2

--- a/solution.py
+++ b/solution.py
@@ -19,7 +19,7 @@
 
 def params(*arrays):
     held = sum(math.prod(shape) * size for shape, size in arrays)
-    return pltpu.CompilerParams(vmem_limit_bytes=min(56 * MIB, held + 6 * MIB))
+    return pltpu.CompilerParams(vmem_limit_bytes=min(56 * MIB, max(24 * MIB, 4 * held)))
 
 
 def pack_kernel(half, place_ref, ids_ref, gates_ref, tokens_ref, cot_ref, *refs):
@@ -261,9 +261,16 @@
 
 
 def sort_kernel(half, wires, slot_ref, flags_ref, *refs):
+    known, refs = refs[:2], refs[2:]
     own_wires, slot_wires = refs[:wires], refs[wires : 2 * wires]
     x_ref, s_ref, wire_ref, sems = refs[2 * wires :]
     rows = half * CAP
+    rest = [
+        pltpu.make_async_copy(
+            source, target.at[:, pl.ds(wires * rows, wires * rows), :], sems.at[wires + n]
+        )
+        for n, (source, target) in enumerate(zip(known, (x_ref, s_ref)))
+    ]
     taken = flags_ref[slot_ref[0] % half] == 1
 
     def fetch(w, source):
@@ -272,6 +279,8 @@
     for w in range(wires):
         pl.when(taken)(functools.partial(fetch, w, slot_wires[w]))
         pl.when(jnp.logical_not(taken))(functools.partial(fetch, w, own_wires[w]))
+    for copy in rest:
+        copy.start()
     order = order_matrix(half, 0)
     for w in range(wires):
         pltpu.make_async_copy(own_wires[w], wire_ref.at[w], sems.at[w]).wait()
@@ -283,34 +292,35 @@
             s_ref[q, pl.ds(w * rows, rows), :] = sorted_rows[
                 (CUTS + q) * rows : (CUTS + q + 1) * rows
             ]
-
-
-def sort_rows(slot, flags, own_wires, slot_wires, half):
+    for copy in rest:
+        copy.wait()
+
+
+def sort_rows(slot, flags, known, own_wires, slot_wires, half):
     count = len(own_wires)
     quarter = own_wires[0].shape[1]
     rows = count * half * CAP
     vmem = pl.BlockSpec(memory_space=pltpu.VMEM)
     hbm = pl.BlockSpec(memory_space=pltpu.HBM)
     smem = pl.BlockSpec(memory_space=pltpu.SMEM)
-    shape = jax.ShapeDtypeStruct((CUTS, rows, quarter), jnp.bfloat16)
+    shape = jax.ShapeDtypeStruct((CUTS, 2 * rows, quarter), jnp.bfloat16)
     return pl.pallas_call(
         functools.partial(sort_kernel, half, count),
         out_shape=(shape, shape),
-        in_specs=[smem, smem] + [hbm] * (2 * count),
+        in_specs=[smem, smem] + [hbm] * (2 + 2 * count),
         out_specs=(vmem, vmem),
         scratch_shapes=[
             pltpu.VMEM((count, half * BLOCK, quarter), jnp.bfloat16),
-            pltpu.SemaphoreType.DMA((count,)),
+            pltpu.SemaphoreType.DMA((count + 2,)),
         ],
-        compiler_params=pltpu.CompilerParams(vmem_limit_bytes=56 * MIB),
+        compiler_params=params(((count,) + own_wires[0].shape, 2), (shape.shape, 2 * 2)),
         name="sort_rows",
-    )(slot, flags, *own_wires, *slot_wires)
+    )(slot, flags, *known, *own_wires, *slot_wires)
 
 
 def grads_kernel(half, parts, slot_ref, flags_ref, *refs):
     own_refs, other_refs = refs[:parts], refs[parts : 2 * parts]
-    x_refs, s_refs = refs[2 * parts : 3 * parts], refs[3 * parts : 4 * parts]
-    gate_ref, up_ref, down_ref, acts_ref, sems = refs[4 * parts :]
+    x_ref, s_ref, gate_ref, up_ref, down_ref, acts_ref, sems = refs[2 * parts :]
     rows = own_refs[0].shape[0]
     hidden_width = gate_ref.shape[1]
 
@@ -328,21 +338,19 @@
             pltpu.make_async_copy(own_refs[p], target, sems.at[p]).wait()
 
     contract = (((0,), (0,)), ((), ()))
-    x = jnp.concatenate([ref[0] for ref in x_refs], axis=0)
-    s = jnp.concatenate([ref[0] for ref in s_refs], axis=0)
     out = lax.dot_general(
-        x, acts_ref[:, hidden_width:], contract, preferred_element_type=jnp.float32
+        x_ref[0], acts_ref[:, hidden_width:], contract, preferred_element_type=jnp.float32
     )
     gate_ref[...] = out[:, :hidden_width].astype(jnp.bfloat16)
     up_ref[...] = out[:, hidden_width:].astype(jnp.bfloat16)
     down_ref[...] = lax.dot_general(
-        acts_ref[:, :hidden_width], s, contract, preferred_element_type=jnp.float32
+        acts_ref[:, :hidden_width], s_ref[0], contract, preferred_element_type=jnp.float32
     ).astype(jnp.bfloat16)
 
 
-def grads(slot, flags, own, other, x_parts, s_parts, half):
+def grads(slot, flags, own, other, x_rows, s_rows, half):
     count = len(own)
-    cuts, rows, quarter = x_parts[0].shape
+    cuts, rows, quarter = x_rows.shape
     width = cuts * quarter
     triple = own[0].shape[1]
     hidden_width = triple // 3
@@ -357,19 +365,19 @@
             jax.ShapeDtypeStruct((width, hidden_width), jnp.bfloat16),
             jax.ShapeDtypeStruct((hidden_width, width), jnp.bfloat16),
         ),
-        in_specs=[smem, smem] + [hbm] * (2 * count) + [part] * (2 * count),
+        in_specs=[smem, smem] + [hbm] * (2 * count) + [part, part],
         out_specs=(
             pl.BlockSpec((quarter, hidden_width), lambda q: (q, 0)),
             pl.BlockSpec((quarter, hidden_width), lambda q: (q, 0)),
             pl.BlockSpec((hidden_width, quarter), lambda q: (0, q)),
         ),
         scratch_shapes=[
-            pltpu.VMEM((count * rows, triple), jnp.bfloat16),
+            pltpu.VMEM((rows, triple), jnp.bfloat16),
             pltpu.SemaphoreType.DMA((count,)),
         ],
-        compiler_params=pltpu.CompilerParams(vmem_limit_bytes=56 * MIB),
+        compiler_params=params(((rows, triple), 2), ((rows, quarter), 8), ((quarter, triple), 4)),
         name="grads",
-    )(slot, flags, *own, *other, *x_parts, *s_parts)
+    )(slot, flags, *own, *other, x_rows, s_rows)
 
 
 def body(tokens, cotangent, expert_ids, gates, swap_flags, gate_w, up_w, down_w):
@@ -428,7 +436,7 @@
     crossed = across(after(home0, slot1), "home_rows_across")
     slots1 = all_planes(slot1, "slot_rows_planes")
     homes1 = all_planes(home1, "crossed_rows_planes")
-    homes1[0] = after(homes1[0], crossed, *slots1[1:])
+    homes1[0] = after(homes1[0], *slots1[1:])
     weights = (gate_w[0], up_w[0], down_w[0])
     acts0, score0 = home(homes0, weights, half)
     slots0 = all_planes(after(crossed, acts0), "slot_crossed_planes")
@@ -436,8 +444,8 @@
         homes1, weights, half, slot, plane, swap_flags, score0, *slots1
     )
     own = [acts0, acts1]
-    other = [across(after(acts0, crossed), "acts_near_across"), across(acts1, "acts_far_across")]
-    x_rows0, s_rows0 = sort_rows(slot, swap_flags, homes0, slots0, half)
+    other = [across(acts0, "acts_near_across"), across(acts1, "acts_far_across")]
+    x_rows, s_rows = sort_rows(slot, swap_flags, (x_rows1, s_rows1), homes0, slots0, half)
 
     returned = lax.all_to_all(
         back.reshape(planes * axis_len, 1, LANES),
@@ -447,7 +455,7 @@
         tiled=True,
     )
     out_gate, out_up, out_down = grads(
-        slot, swap_flags, own, other, [x_rows0, x_rows1], [s_rows0, s_rows1], half
+        slot, swap_flags, own, other, x_rows, s_rows, half
     )
     returned = after(returned, out_down)
     total = jnp.sum(returned.reshape(planes, axis_len, LANES), axis=0)

time: 124 us -> 124 us (level)
  waiting for transfers between devices: 57.5 us -> 52.4 us
  local copies, waits for them, and re-layouts: 2.84 us -> 6.96 us
  Pallas kernels: 33.5 us -> 29.9 us
  starting transfers between devices: 28 us -> 31.6 us
    ppermute x8, waiting for transfers between devices: 26.9 us -> 21.1 us  [flip(): return lax.ppermute(block, 'expert', [(i, i ^ by) for i in range(axis_len)])]
    unnamed x23 -> x29, local copies, waits for them, and re-layouts: 1.66 us -> 5.12 us
    all_to_all x1, starting transfers between devices: 2.85 us -> 5.6 us  [body(): lax.all_to_all(back.reshape(planes * axis_len, 1, LANES), ('dp', 'expert'...]
    pallas_call x1, Pallas kernels: 8.26 us -> 6.1 us  [grads(): pl.pallas_call(functools.partial(grads_kernel, half, count), grid=(cuts,)...]
  transfers between devices with their start and end apart: 15 -> 15, of which waited for: 10 -> 10; matrix products, arithmetic and copies ran while one was open for 1% -> 3% of each run, Pallas kernels for 23% -> 20%
where the time goes in v3:
time: 124 us; the launch traced here: 123 us
  waiting for transfers between devices  52.4 us (42%)
  starting transfers between devices  31.6 us (25%)
  Pallas kernels  29.9 us (24%)
  local copies, waits for them, and re-layouts  6.96 us (6%)
    all_to_all x2, waiting for transfers between devices, exchange(): lax.all_to_all(blocks, 'expert', split_axis=0, concat_axis=0, tiled=True,...  27 us
    ppermute x8, waiting for transfers between devices, flip(): return lax.ppermute(block, 'expert', [(i, i ^ by) for i in range(axis_len)])  21.1 us
    pallas_call x2, Pallas kernels, home(): pl.pallas_call(functools.partial(home_kernel, half, count, bool(more)), o...  15.5 us
    ppermute x8, starting transfers between devices, flip(): return lax.ppermute(block, 'expert', [(i, i ^ by) for i in range(axis_len)])  10.7 us
    all_to_all x2, starting transfers between devices, exchange(): lax.all_to_all(blocks, 'expert', split_axis=0, concat_axis=0, tiled=True,...  9.48 us
    pallas_call x1, Pallas kernels, grads(): pl.pallas_call(functools.partial(grads_kernel, half, count), grid=(cuts,)...  6.1 us
    ppermute x4, starting transfers between devices, all_planes(): lax.ppermute(wire, 'dp', [(i, (i + by) % planes) for i in range(planes)])  5.91 us
    all_to_all x1, starting transfers between devices, body(): lax.all_to_all(back.reshape(planes * axis_len, 1, LANES), ('dp', 'expert'...  5.6 us
  transfers between devices with their start and end apart: 15, of which 10 were waited for; matrix products, arithmetic and copies ran while one was open for 3% of the time, Pallas kernels for 20%

profile of v3, /device:TPU:0, one launch (start us, length us, event | category | flops | bytes accessed | tf_op | source)
XLA Modules:
  0.0 122.5 jit_solution(10121419853954535534)
XLA Ops:
  0.6 5.3 %pack.1 = (bf16[384,896]{1,0:T(8,128)(2,1)}, bf16[384,896]{1,0:T(8,128)(2,1)}, bf16[192,896]{1,0:T(8,128)(2,1)}, bf16[192,896]{1,0:T(8,128)(2,1)}, s32[8,128]{1,0:T(8,128)}) custom-call(s32[1]{0:T(128)} %bitcast.place_ref.refs_0_.slot_ref, s32[8,128]{1,0:T(8,128)} %bitcast.38, bf16[8,128]{1,0:T(8,128)(2,1)} %bitcast.37, bf16[128,3584]{1,0:T(8,128)(2,1)} %tokens_ref.1, ...), custom_call_target="tpu_custom_call" | custom-call | tf_op jit(solution)/shard_map/pack/pallas_call | solution.py:102
  6.0 5.3 %all-to-all-start = ((bf16[8,48,896]{2,1,0:T(8,128)(2,1)}), bf16[8,48,896]{2,1,0:T(8,128)(2,1)S(1)}, u32[]{:S(2)}, u32[]{:S(2)}) async-start(bf16[8,48,896]{2,1,0:T(8,128)(2,1)} %bitcast.33), calls=%async_computation | async-start | bytes 1376256 | tf_op jit(solution)/shard_map/home_rows_half/all_to_all | solution.py:396
  11.3 0.5 collective-permute-start.1
  11.8 2.6 %collective-permute-start.6 = (bf16[384,896]{1,0:T(8,128)(2,1)}, bf16[384,896]{1,0:T(8,128)(2,1)}, u32[]{:S(2)}, u32[]{:S(2)}) collective-permute-start(bf16[384,896]{1,0:T(8,128)(2,1)} %get-tuple-element.38), channel_id=1, source_target_pairs={{0,8},{1,9},{2,10},{3,11},{4,12},{5,13},{6,14},{7,15},{8,0},{9,1},... | collective-permute-start | bytes 2064392 | tf_op jit(solution)/shard_map/rows_across/ppermute | solution.py:403
  14.4 1.0 fusion
  15.4 0.0 collective-permute-done.1
  15.5 1.7 %collective-permute-start.2 = (bf16[96,896]{1,0:T(8,128)(2,1)S(1)}, bf16[96,896]{1,0:T(8,128)(2,1)S(1)}, u32[]{:S(2)}, u32[]{:S(2)}) collective-permute-start(bf16[96,896]{1,0:T(8,128)(2,1)S(1)} %pad_maximum_fusion.1), channel_id=1, source_target_pairs={{0,2},{1,3},{2,0},{3,1},{4,6},{5,7},{6,4},{7,5},{8,10},{9,11},{10,... | collective-permute-start | bytes 516104 | tf_op jit(solution)/shard_map/slot_rows_chips1/ppermute | solution.py:403
  17.2 1.5 %collective-permute-start.3 = (bf16[96,896]{1,0:T(8,128)(2,1)S(1)}, bf16[96,896]{1,0:T(8,128)(2,1)S(1)}, u32[]{:S(2)}, u32[]{:S(2)}) collective-permute-start(bf16[96,896]{1,0:T(8,128)(2,1)S(1)} %pad_maximum_fusion.2), channel_id=1, source_target_pairs={{0,4},{1,5},{2,6},{3,7},{4,0},{5,1},{6,2},{7,3},{8,12},{9,13},{10,... | collective-permute-start | bytes 516104 | tf_op jit(solution)/shard_map/slot_rows_chips2/ppermute | solution.py:403
  18.8 12.0 %all-to-all-done = bf16[8,48,896]{2,1,0:T(8,128)(2,1)S(1)} async-done(((bf16[8,48,896]{2,1,0:T(8,128)(2,1)}), bf16[8,48,896]{2,1,0:T(8,128)(2,1)S(1)}, u32[]{:S(2)}, u32[]{:S(2)}) %all-to-all-start) | async-done | bytes 688160 | tf_op jit(solution)/shard_map/home_rows_half/all_to_all | solution.py:396
  30.8 1.5 %collective-permute-start = (bf16[384,896]{1,0:T(8,128)(2,1)S(1)}, bf16[384,896]{1,0:T(8,128)(2,1)S(1)}, u32[]{:S(2)}, u32[]{:S(2)}) collective-permute-start(bf16[384,896]{1,0:T(8,128)(2,1)S(1)} %bitcast.23), channel_id=1, source_target_pairs={{0,16},{16,0},{1,17},{17,1},{2,18},{18,2},{3,19},{19,3},{4,20},{20... | collective-permute-start | bytes 2064392 | tf_op jit(solution)/shard_map/home_rows_planes/ppermute | solution.py:420
  32.3 0.1 collective-permute-start.4
  32.4 0.0 collective-permute-done.2
  32.4 6.0 %collective-permute-done.3 = bf16[96,896]{1,0:T(8,128)(2,1)S(1)} collective-permute-done((bf16[96,896]{1,0:T(8,128)(2,1)S(1)}, bf16[96,896]{1,0:T(8,128)(2,1)S(1)}, u32[]{:S(2)}, u32[]{:S(2)}) %collective-permute-start.3) | collective-permute-done | bytes 172064 | tf_op jit(solution)/shard_map/slot_rows_chips2/ppermute | solution.py:403
  38.4 3.5 %collective-permute-done.4 = bf16[96,896]{1,0:T(8,128)(2,1)S(1)} collective-permute-done((bf16[96,896]{1,0:T(8,128)(2,1)S(1)}, bf16[96,896]{1,0:T(8,128)(2,1)S(1)}, u32[]{:S(2)}, u32[]{:S(2)}) %collective-permute-start.4) | collective-permute-done | bytes 172064 | tf_op jit(solution)/shard_map/slot_rows_chips3/ppermute | solution.py:403
  42.0 0.7 constant_dynamic-update-slice_fusion.3
  42.6 0.7 constant_dynamic-update-slice_fusion.2
  43.3 0.7 constant_dynamic-update-slice_fusion.1
  44.0 0.7 constant_dynamic-update-slice_fusion.refs_4_
  44.7 0.4 collective-permute-done.6
  45.1 2.3 %collective-permute-done.refs_1_.refs_3_ = bf16[384,896]{1,0:T(8,128)(2,1)S(1)} collective-permute-done((bf16[384,896]{1,0:T(8,128)(2,1)S(1)}, bf16[384,896]{1,0:T(8,128)(2,1)S(1)}, u32[]{:S(2)}, u32[]{:S(2)}) %collective-permute-start) | collective-permute-done | bytes 688160 | tf_op jit(solution)/shard_map/home_rows_planes/ppermute | solution.py:420
  47.4 4.2 %all-to-all-start.1 = ((bf16[8,48,896]{2,1,0:T(8,128)(2,1)}), bf16[8,48,896]{2,1,0:T(8,128)(2,1)}, u32[]{:S(2)}, u32[]{:S(2)}) async-start(bf16[8,48,896]{2,1,0:T(8,128)(2,1)} %bitcast.9), calls=%async_computation.1 | async-start | bytes 1376256 | tf_op jit(solution)/shard_map/crossed_rows_half/all_to_all | solution.py:396
  51.6 2.9 %collective-permute-start.10 = (bf16[384,896]{1,0:T(8,128)(2,1)S(1)}, bf16[384,896]{1,0:T(8,128)(2,1)S(1)}, u32[]{:S(2)}, u32[]{:S(2)}) collective-permute-start(bf16[384,896]{1,0:T(8,128)(2,1)S(1)} %bitcast.24), channel_id=1, source_target_pairs={{0,8},{1,9},{2,10},{3,11},{4,12},{5,13},{6,14},{7,15},{8,0},{9,1},... | collective-permute-start | bytes 2064392 | tf_op jit(solution)/shard_map/home_rows_across/ppermute | solution.py:403
  54.6 1.5 %collective-permute-start.5 = (bf16[384,896]{1,0:T(8,128)(2,1)}, bf16[384,896]{1,0:T(8,128)(2,1)S(1)}, u32[]{:S(2)}, u32[]{:S(2)}) collective-permute-start(bf16[384,896]{1,0:T(8,128)(2,1)} %constant_dynamic-update-slice_fusion.refs_4_), channel_id=1, source_target_pairs={{0,16},{16,0},{1,17},{17,1},{2,18},{18,2},{3,19},{19,3},{4,20},{20... | collective-permute-start | bytes 2064392 | tf_op jit(solution)/shard_map/slot_rows_planes/ppermute | solution.py:420
  56.0 15.0 %all-to-all-done.1 = bf16[8,48,896]{2,1,0:T(8,128)(2,1)} async-done(((bf16[8,48,896]{2,1,0:T(8,128)(2,1)}), bf16[8,48,896]{2,1,0:T(8,128)(2,1)}, u32[]{:S(2)}, u32[]{:S(2)}) %all-to-all-start.1) | async-done | bytes 688160 | tf_op jit(solution)/shard_map/crossed_rows_half/all_to_all | solution.py:396
  71.0 1.5 %collective-permute-start.7 = (bf16[384,896]{1,0:T(8,128)(2,1)}, bf16[384,896]{1,0:T(8,128)(2,1)S(1)}, u32[]{:S(2)}, u32[]{:S(2)}) collective-permute-start(bf16[384,896]{1,0:T(8,128)(2,1)} %bitcast.10.refs_6_), channel_id=1, source_target_pairs={{0,16},{16,0},{1,17},{17,1},{2,18},{18,2},{3,19},{19,3},{4,20},{20... | collective-permute-start | bytes 2064392 | tf_op jit(solution)/shard_map/crossed_rows_planes/ppermute | solution.py:420
  72.5 0.0 copy-done
  72.5 7.5 %home.1 = (bf16[96,1536]{1,0:T(8,128)(2,1)}, f32[16,128]{1,0:T(8,128)}) custom-call(bf16[384,896]{1,0:T(8,128)(2,1)} %bitcast.25, bf16[384,896]{1,0:T(8,128)(2,1)} %copy-done.2, bf16[3584,512]{1,0:T(8,128)(2,1)} %bitcast.27, bf16[3584,512]{1,0:T(8,128)(2,1)} %bitcast.29, bf16[512,3584]{1,0:T(8,128)(2,1)} %bitcast.31), custom_call_target="tpu_custom_call" | custom-call | tf_op jit(solution)/shard_map/home/pallas_call | solution.py:249
  80.0 5.3 %collective-permute-done.10.refs_4_ = bf16[384,896]{1,0:T(8,128)(2,1)S(1)} collective-permute-done((bf16[384,896]{1,0:T(8,128)(2,1)S(1)}, bf16[384,896]{1,0:T(8,128)(2,1)S(1)}, u32[]{:S(2)}, u32[]{:S(2)}) %collective-permute-start.10) | collective-permute-done | bytes 688160 | tf_op jit(solution)/shard_map/home_rows_across/ppermute | solution.py:403
  85.3 1.5 %collective-permute-start.11 = (bf16[384,896]{1,0:T(8,128)(2,1)S(1)}, bf16[384,896]{1,0:T(8,128)(2,1)S(1)}, u32[]{:S(2)}, u32[]{:S(2)}) collective-permute-start(bf16[384,896]{1,0:T(8,128)(2,1)S(1)} %collective-permute-done.10.refs_4_), channel_id=1, source_target_pairs={{0,16},{16,0},{1,17},{17,1},{2,18},{18,2},{3,19},{19,3},{4,20},{20... | collective-permute-start | bytes 2064392 | tf_op jit(solution)/shard_map/slot_crossed_planes/ppermute | solution.py:420
  86.7 0.0 collective-permute-start.8
  86.8 0.0 collective-permute-done.5.refs_5_
  86.8 1.9 %collective-permute-done.7.refs_7_ = bf16[384,896]{1,0:T(8,128)(2,1)S(1)} collective-permute-done((bf16[384,896]{1,0:T(8,128)(2,1)}, bf16[384,896]{1,0:T(8,128)(2,1)S(1)}, u32[]{:S(2)}, u32[]{:S(2)}) %collective-permute-start.7) | collective-permute-done | bytes 688160 | tf_op jit(solution)/shard_map/crossed_rows_planes/ppermute | solution.py:420
  88.7 0.0 copy-done.9
  88.7 0.8 copy-done.10
  89.6 8.0 %home_last.1 = (bf16[96,1536]{1,0:T(8,128)(2,1)}, f32[32,128]{1,0:T(8,128)}, bf16[4,96,896]{2,1,0:T(8,128)(2,1)}, bf16[4,96,896]{2,1,0:T(8,128)(2,1)}) custom-call(s32[1]{0:T(128)} %bitcast.place_ref.refs_0_.slot_ref, s32[1]{0:T(128)} %bitcast.8.refs_1_, s32[8]{0:T(128)} %flags_ref.3, f32[16,128]{1,0:T(8,128)} %get-tuple-element.31.refs_3_, ...), custom_call_target="tpu_custom_call" | custom-call | tf_op jit(solution)/shard_map/home_last/pallas_call | solution.py:249
  97.6 1.3 %collective-permute-start.9 = (bf16[96,1536]{1,0:T(8,128)(2,1)}, bf16[96,1536]{1,0:T(8,128)(2,1)}, u32[]{:S(2)}, u32[]{:S(2)}) collective-permute-start(bf16[96,1536]{1,0:T(8,128)(2,1)} %get-tuple-element.41.refs_1_), channel_id=1, source_target_pairs={{0,8},{1,9},{2,10},{3,11},{4,12},{5,13},{6,14},{7,15},{8,0},{9,1},... | collective-permute-start | bytes 884744 | tf_op jit(solution)/shard_map/acts_far_across/ppermute | solution.py:403
  98.8 5.6 %all-to-all-start.2 = ((f32[32,1,128]{2,1,0:T(1,128)}), f32[32,1,128]{2,1,0:T(1,128)S(1)}, u32[]{:S(2)}, u32[]{:S(2)}) async-start(f32[32,1,128]{2,1,0:T(1,128)} %bitcast.36), calls=%async_computation.2 | async-start | bytes 32768 | tf_op jit(solution)/shard_map/all_to_all | solution.py:450
  104.5 0.0 collective-permute-done.11.refs_5_
  104.5 1.1 copy-done.4
  105.6 1.1 copy-done.5
  106.7 3.0 %sort_rows.1 = (bf16[4,192,896]{2,1,0:T(8,128)(2,1)S(1)}, bf16[4,192,896]{2,1,0:T(8,128)(2,1)S(1)}) custom-call(s32[1]{0:T(128)} %bitcast.place_ref.refs_0_.slot_ref, s32[8]{0:T(128)S(1)} %copy-done.8, bf16[4,96,896]{2,1,0:T(8,128)(2,1)S(1)} %copy-done.4, bf16[4,96,896]{2,1,0:T(8,128)(2,1)S(1)} %copy-done.5, bf16[384,896]{1,0:T(8,128)(2,1)S(1)} %bitcast.26, ...), custom_call_target="tpu_custom_call" | custom-call | tf_op jit(solution)/shard_map/sort_rows/pallas_call | solution.py:307
  109.7 0.2 collective-permute-done.8.refs_2_
  109.9 5.7 %collective-permute-done.9.refs_3_ = bf16[96,1536]{1,0:T(8,128)(2,1)} collective-permute-done((bf16[96,1536]{1,0:T(8,128)(2,1)}, bf16[96,1536]{1,0:T(8,128)(2,1)}, u32[]{:S(2)}, u32[]{:S(2)}) %collective-permute-start.9) | collective-permute-done | bytes 294944 | tf_op jit(solution)/shard_map/acts_far_across/ppermute | solution.py:403
  115.6 6.1 %grads.1 = (bf16[3584,512]{1,0:T(8,128)(2,1)}, bf16[3584,512]{1,0:T(8,128)(2,1)}, bf16[512,3584]{1,0:T(8,128)(2,1)}) custom-call(s32[1]{0:T(128)} %bitcast.place_ref.refs_0_.slot_ref, s32[8]{0:T(128)S(1)} %copy-done.8, bf16[96,1536]{1,0:T(8,128)(2,1)S(1)} %copy-done.6, bf16[96,1536]{1,0:T(8,128)(2,1)S(1)} %copy-done.7, ...), custom_call_target="tpu_custom_call" | custom-call | tf_op jit(solution)/shard_map/grads/pallas_call | solution.py:360
  121.7 0.0 all-to-all-done.2
  121.7 0.1 broadcast_in_dim.28
  121.8 0.1 select_reduce_fusion
  121.9 0.6 bitcast_divide_fusion
  (27 shorter events, 0.1 us)
Async XLA Ops:
  6.0 24.8 %all-to-all-start = ((bf16[8,48,896]{2,1,0:T(8,128)(2,1)}), bf16[8,48,896]{2,1,0:T(8,128)(2,1)S(1)}, u32[]{:S(2)}, u32[]{:S(2)}) async-start(bf16[8,48,896]{2,1,0:T(8,128)(2,1)} %bitcast.33), calls=%async_computation | async-start | bytes 1376256 | tf_op jit(solution)/shard_map/home_rows_half/all_to_all | solution.py:396
  11.3 4.2 %collective-permute-start.1 = (bf16[192,896]{1,0:T(8,128)(2,1)}, bf16[192,896]{1,0:T(8,128)(2,1)S(1)}, u32[]{:S(2)}, u32[]{:S(2)}) collective-permute-start(bf16[192,896]{1,0:T(8,128)(2,1)} %get-tuple-element.33), channel_id=1, source_target_pairs={{0,1},{1,0},{2,3},{3,2},{4,5},{5,4},{6,7},{7,6},{8,9},{9,8},{10,11... | collective-permute-start | bytes 1032200 | tf_op jit(solution)/shard_map/slot_rows_cores/ppermute | solution.py:403
  11.8 33.3 %collective-permute-start.6 = (bf16[384,896]{1,0:T(8,128)(2,1)}, bf16[384,896]{1,0:T(8,128)(2,1)}, u32[]{:S(2)}, u32[]{:S(2)}) collective-permute-start(bf16[384,896]{1,0:T(8,128)(2,1)} %get-tuple-element.38), channel_id=1, source_target_pairs={{0,8},{1,9},{2,10},{3,11},{4,12},{5,13},{6,14},{7,15},{8,0},{9,1},... | collective-permute-start | bytes 2064392 | tf_op jit(solution)/shard_map/rows_across/ppermute | solution.py:403
  15.5 16.9 %collective-permute-start.2 = (bf16[96,896]{1,0:T(8,128)(2,1)S(1)}, bf16[96,896]{1,0:T(8,128)(2,1)S(1)}, u32[]{:S(2)}, u32[]{:S(2)}) collective-permute-start(bf16[96,896]{1,0:T(8,128)(2,1)S(1)} %pad_maximum_fusion.1), channel_id=1, source_target_pairs={{0,2},{1,3},{2,0},{3,1},{4,6},{5,7},{6,4},{7,5},{8,10},{9,11},{10,... | collective-permute-start | bytes 516104 | tf_op jit(solution)/shard_map/slot_rows_chips1/ppermute | solution.py:403
  17.2 21.2 %collective-permute-start.3 = (bf16[96,896]{1,0:T(8,128)(2,1)S(1)}, bf16[96,896]{1,0:T(8,128)(2,1)S(1)}, u32[]{:S(2)}, u32[]{:S(2)}) collective-permute-start(bf16[96,896]{1,0:T(8,128)(2,1)S(1)} %pad_maximum_fusion.2), channel_id=1, source_target_pairs={{0,4},{1,5},{2,6},{3,7},{4,0},{5,1},{6,2},{7,3},{8,12},{9,13},{10,... | collective-permute-start | bytes 516104 | tf_op jit(solution)/shard_map/slot_rows_chips2/ppermute | solution.py:403
  30.8 41.7 %copy-start = (bf16[8,48,896]{2,1,0:T(8,128)(2,1)}, bf16[8,48,896]{2,1,0:T(8,128)(2,1)S(1)}, u32[]{:S(2)}) copy-start(bf16[8,48,896]{2,1,0:T(8,128)(2,1)S(1)} %all-to-all-done) | copy-start | bytes 2064388
  30.8 16.6 %collective-permute-start = (bf16[384,896]{1,0:T(8,128)(2,1)S(1)}, bf16[384,896]{1,0:T(8,128)(2,1)S(1)}, u32[]{:S(2)}, u32[]{:S(2)}) collective-permute-start(bf16[384,896]{1,0:T(8,128)(2,1)S(1)} %bitcast.23), channel_id=1, source_target_pairs={{0,16},{16,0},{1,17},{17,1},{2,18},{18,2},{3,19},{19,3},{4,20},{20... | collective-permute-start | bytes 2064392 | tf_op jit(solution)/shard_map/home_rows_planes/ppermute | solution.py:420
  32.3 9.6 %collective-permute-start.4 = (bf16[96,896]{1,0:T(8,128)(2,1)S(1)}, bf16[96,896]{1,0:T(8,128)(2,1)S(1)}, u32[]{:S(2)}, u32[]{:S(2)}) collective-permute-start(bf16[96,896]{1,0:T(8,128)(2,1)S(1)} %pad_maximum_fusion.3), channel_id=1, source_target_pairs={{0,6},{1,7},{2,4},{3,5},{4,2},{5,3},{6,0},{7,1},{8,14},{9,15},{10,... | collective-permute-start | bytes 516104 | tf_op jit(solution)/shard_map/slot_rows_chips3/ppermute | solution.py:403
  47.4 25.1 %copy-start.2 = (bf16[384,896]{1,0:T(8,128)(2,1)}, bf16[384,896]{1,0:T(8,128)(2,1)S(1)}, u32[]{:S(2)}) copy-start(bf16[384,896]{1,0:T(8,128)(2,1)S(1)} %collective-permute-done.refs_1_.refs_3_) | copy-start | bytes 2064388
  47.4 23.6 %all-to-all-start.1 = ((bf16[8,48,896]{2,1,0:T(8,128)(2,1)}), bf16[8,48,896]{2,1,0:T(8,128)(2,1)}, u32[]{:S(2)}, u32[]{:S(2)}) async-start(bf16[8,48,896]{2,1,0:T(8,128)(2,1)} %bitcast.9), calls=%async_computation.1 | async-start | bytes 1376256 | tf_op jit(solution)/shard_map/crossed_rows_half/all_to_all | solution.py:396
  51.6 33.6 %collective-permute-start.10 = (bf16[384,896]{1,0:T(8,128)(2,1)S(1)}, bf16[384,896]{1,0:T(8,128)(2,1)S(1)}, u32[]{:S(2)}, u32[]{:S(2)}) collective-permute-start(bf16[384,896]{1,0:T(8,128)(2,1)S(1)} %bitcast.24), channel_id=1, source_target_pairs={{0,8},{1,9},{2,10},{3,11},{4,12},{5,13},{6,14},{7,15},{8,0},{9,1},... | collective-permute-start | bytes 2064392 | tf_op jit(solution)/shard_map/home_rows_across/ppermute | solution.py:403
  54.6 32.2 %collective-permute-start.5 = (bf16[384,896]{1,0:T(8,128)(2,1)}, bf16[384,896]{1,0:T(8,128)(2,1)S(1)}, u32[]{:S(2)}, u32[]{:S(2)}) collective-permute-start(bf16[384,896]{1,0:T(8,128)(2,1)} %constant_dynamic-update-slice_fusion.refs_4_), channel_id=1, source_target_pairs={{0,16},{16,0},{1,17},{17,1},{2,18},{18,2},{3,19},{19,3},{4,20},{20... | collective-permute-start | bytes 2064392 | tf_op jit(solution)/shard_map/slot_rows_planes/ppermute | solution.py:420
  71.0 17.7 %collective-permute-start.7 = (bf16[384,896]{1,0:T(8,128)(2,1)}, bf16[384,896]{1,0:T(8,128)(2,1)S(1)}, u32[]{:S(2)}, u32[]{:S(2)}) collective-permute-start(bf16[384,896]{1,0:T(8,128)(2,1)} %bitcast.10.refs_6_), channel_id=1, source_target_pairs={{0,16},{16,0},{1,17},{17,1},{2,18},{18,2},{3,19},{19,3},{4,20},{20... | collective-permute-start | bytes 2064392 | tf_op jit(solution)/shard_map/crossed_rows_planes/ppermute | solution.py:420
  85.3 19.2 %collective-permute-start.11 = (bf16[384,896]{1,0:T(8,128)(2,1)S(1)}, bf16[384,896]{1,0:T(8,128)(2,1)S(1)}, u32[]{:S(2)}, u32[]{:S(2)}) collective-permute-start(bf16[384,896]{1,0:T(8,128)(2,1)S(1)} %collective-permute-done.10.refs_4_), channel_id=1, source_target_pairs={{0,16},{16,0},{1,17},{17,1},{2,18},{18,2},{3,19},{19,3},{4,20},{20... | collective-permute-start | bytes 2064392 | tf_op jit(solution)/shard_map/slot_crossed_planes/ppermute | solution.py:420
  86.7 23.2 %collective-permute-start.8 = (bf16[96,1536]{1,0:T(8,128)(2,1)}, bf16[96,1536]{1,0:T(8,128)(2,1)S(1)}, u32[]{:S(2)}, u32[]{:S(2)}) collective-permute-start(bf16[96,1536]{1,0:T(8,128)(2,1)} %get-tuple-element.30.refs_0_), channel_id=1, source_target_pairs={{0,8},{1,9},{2,10},{3,11},{4,12},{5,13},{6,14},{7,15},{8,0},{9,1},... | collective-permute-start | bytes 884744 | tf_op jit(solution)/shard_map/acts_near_across/ppermute | solution.py:403
  86.8 2.0 %copy-start.9 = (bf16[384,896]{1,0:T(8,128)(2,1)}, bf16[384,896]{1,0:T(8,128)(2,1)S(1)}, u32[]{:S(2)}) copy-start(bf16[384,896]{1,0:T(8,128)(2,1)S(1)} %collective-permute-done.5.refs_5_) | copy-start | bytes 2064388
  88.7 0.8 copy-start.10
  89.5 14.9 %copy-start.1 = (bf16[8,48,896]{2,1,0:T(8,128)(2,1)S(1)}, bf16[8,48,896]{2,1,0:T(8,128)(2,1)}, u32[]{:S(2)}) copy-start(bf16[8,48,896]{2,1,0:T(8,128)(2,1)} %copy-done) | copy-start | bytes 2064388
  89.6 14.9 %copy-start.3 = (bf16[384,896]{1,0:T(8,128)(2,1)S(1)}, bf16[384,896]{1,0:T(8,128)(2,1)}, u32[]{:S(2)}) copy-start(bf16[384,896]{1,0:T(8,128)(2,1)} %copy-done.2) | copy-start | bytes 2064388
  89.6 14.9 %copy-start.8 = (s32[8]{0:T(128)S(1)}, s32[8]{0:T(128)}, u32[]{:S(2)}) copy-start(s32[8]{0:T(128)} %flags_ref.3) | copy-start | bytes 100
  89.6 26.0 %copy-start.6 = (bf16[96,1536]{1,0:T(8,128)(2,1)S(1)}, bf16[96,1536]{1,0:T(8,128)(2,1)}, u32[]{:S(2)}) copy-start(bf16[96,1536]{1,0:T(8,128)(2,1)} %get-tuple-element.30.refs_0_) | copy-start | bytes 884740
  97.6 18.0 %collective-permute-start.9 = (bf16[96,1536]{1,0:T(8,128)(2,1)}, bf16[96,1536]{1,0:T(8,128)(2,1)}, u32[]{:S(2)}, u32[]{:S(2)}) collective-permute-start(bf16[96,1536]{1,0:T(8,128)(2,1)} %get-tuple-element.41.refs_1_), channel_id=1, source_target_pairs={{0,8},{1,9},{2,10},{3,11},{4,12},{5,13},{6,14},{7,15},{8,0},{9,1},... | collective-permute-start | bytes 884744 | tf_op jit(solution)/shard_map/acts_far_across/ppermute | solution.py:403
  98.8 22.8 %all-to-all-start.2 = ((f32[32,1,128]{2,1,0:T(1,128)}), f32[32,1,128]{2,1,0:T(1,128)S(1)}, u32[]{:S(2)}, u32[]{:S(2)}) async-start(f32[32,1,128]{2,1,0:T(1,128)} %bitcast.36), calls=%async_computation.2 | async-start | bytes 32768 | tf_op jit(solution)/shard_map/all_to_all | solution.py:450
  104.5 1.1 copy-start.4
  105.6 1.1 copy-start.5
  106.7 8.9 %copy-start.7 = (bf16[96,1536]{1,0:T(8,128)(2,1)S(1)}, bf16[96,1536]{1,0:T(8,128)(2,1)}, u32[]{:S(2)}) copy-start(bf16[96,1536]{1,0:T(8,128)(2,1)} %get-tuple-element.41.refs_1_) | copy-start | bytes 884740
  106.7 15.1 %copy-start.12 = (s32[8,128]{1,0:T(8,128)S(1)}, s32[8,128]{1,0:T(8,128)}, u32[]{:S(2)}) copy-start(s32[8,128]{1,0:T(8,128)} %get-tuple-element.51) | copy-start | bytes 12292
  106.7 15.2 %copy-start.11 = (bf16[128,8]{0,1:T(8,128)(2,1)S(1)}, bf16[128,8]{0,1:T(8,128)(2,1)}, u32[]{:S(2)}) copy-start(bf16[128,8]{0,1:T(8,128)(2,1)} %param.11) | copy-start | bytes 6148
